TPU v7x, 256 devices: a whole 4x4x8 slice. The times are simulated.
256 devices in a mesh: ctx: 32 (over y, x, core), head: 8 (over z).
Axes of the slice: x: 4, y: 4, z: 8, core: 2. Of those that a mesh axis runs over, the one named last changes fastest.
Arguments:
- queries: bfloat16 [4096, 8192], P('ctx', 'head'), may hold values from -90 to 90
- keys: bfloat16 [4096, 1024], P('ctx', 'head'), may hold values from -4 to 4
- values: bfloat16 [4096, 1024], P('ctx', 'head'), may hold values from -5 to 5
- out_grad: bfloat16 [4096, 8192], P('ctx', 'head'), may hold values from -5 to 5
- block_order: int32 [64], replicated, may hold values from 0 to 63, each once
Outputs:
- grads: bfloat16 [4096, 10240], P(('ctx', 'head'))
All inputs are finite; a program needn't handle non-finite values.
Results may differ from a plain program's by a relative error of at most 0.006.
Values may be sent and summed in bfloat16 or wider, within the bound.
No kernel may reach another device: no remote copies, remote signals or barrier semaphores. Data moves between devices by JAX's collectives and lax.ppermute only.
A program may use at most 64 MiB of HBM per device.

v0:
```python
import math

import jax
import jax.numpy as jnp
from jax import lax
from jax.sharding import PartitionSpec as P

HD = 128
QGROUP = 8


NEG = -1e30


def positions_of(rows, block_order, block_len):
    slots = rows // block_len
    table = jnp.arange(block_order.shape[0], dtype=jnp.int32)
    starts = jnp.sum(jnp.where(slots[:, None] == table[None, :], block_order[None, :], 0), axis=1)
    return starts * block_len + rows % block_len


def shards(queries, keys, values, out_grad, block_order):
    tok_rows = queries.shape[0]
    local_kv = keys.shape[1] // HD
    score_scale = HD ** (-0.5)
    ctx_count = lax.axis_size("ctx")
    seq_total = tok_rows * ctx_count
    block_len = tok_rows // 2
    key_all, value_all = (
        lax.all_gather(keys, "ctx", axis=0, tiled=True),
        lax.all_gather(values, "ctx", axis=0, tiled=True),
    )
    own_rows = lax.axis_index("ctx") * tok_rows + jnp.arange(tok_rows, dtype=jnp.int32)
    query_pos = positions_of(own_rows, block_order, block_len)
    key_pos = positions_of(jnp.arange(seq_total, dtype=jnp.int32), block_order, block_len)
    query_heads = queries.reshape(tok_rows, local_kv, QGROUP, HD)
    grad_heads = out_grad.reshape(tok_rows, local_kv, QGROUP, HD)
    key_block = math.gcd(512, seq_total)
    block_count = seq_total // key_block
    key_blocks = key_all.reshape(block_count, key_block, local_kv, HD)
    value_blocks = value_all.reshape(block_count, key_block, local_kv, HD)
    pos_blocks = key_pos.reshape(block_count, key_block)

    def scores(key_part, pos_part):
        score = (
            jnp.einsum("igqd,jgd->gqij", query_heads, key_part, preferred_element_type=jnp.float32)
            * score_scale
        )
        allowed = pos_part[None, :] <= query_pos[:, None]
        return jnp.where(allowed[None, None], score, NEG)

    def stats_step(carry, inputs):
        row_top, row_total = carry
        key_part, pos_part = inputs
        score = scores(key_part, pos_part)
        new_top = jnp.maximum(row_top, jnp.max(score, axis=-1))
        row_total = row_total * jnp.exp(row_top - new_top) + jnp.sum(
            jnp.exp(score - new_top[..., None]), axis=-1
        )
        return ((new_top, row_total), None)

    start_shape = (local_kv, QGROUP, tok_rows)
    (row_top, row_total), unused = lax.scan(
        stats_step,
        (jnp.full(start_shape, NEG, jnp.float32), jnp.zeros(start_shape, jnp.float32)),
        (key_blocks, pos_blocks),
    )
    log_total = row_top + jnp.log(row_total)

    def probs_and_grads(key_part, value_part, pos_part):
        attn_probs = jnp.exp(scores(key_part, pos_part) - log_total[..., None])
        grad_probs = jnp.einsum(
            "igqd,jgd->gqij", grad_heads, value_part, preferred_element_type=jnp.float32
        )
        return (attn_probs, grad_probs)

    def delta_step(carry, inputs):
        attn_probs, grad_probs = probs_and_grads(*inputs)
        return (carry + jnp.sum(attn_probs * grad_probs, axis=-1), None)

    row_delta, unused = lax.scan(
        delta_step, jnp.zeros(start_shape, jnp.float32), (key_blocks, value_blocks, pos_blocks)
    )

    def grad_step(carry, inputs):
        key_part = inputs[0]
        attn_probs, grad_probs = probs_and_grads(*inputs)
        grad_score = (attn_probs * (grad_probs - row_delta[..., None]) * score_scale).astype(
            jnp.bfloat16
        )
        probs_low = attn_probs.astype(jnp.bfloat16)
        carry = carry + jnp.einsum(
            "gqij,jgd->igqd", grad_score, key_part, preferred_element_type=jnp.float32
        )
        grad_key = jnp.einsum(
            "gqij,igqd->jgd", grad_score, query_heads, preferred_element_type=jnp.float32
        )
        grad_value = jnp.einsum(
            "gqij,igqd->jgd", probs_low, grad_heads, preferred_element_type=jnp.float32
        )
        return (carry, (grad_key, grad_value))

    grad_query, (key_parts, value_parts) = lax.scan(
        grad_step,
        jnp.zeros((tok_rows, local_kv, QGROUP, HD), jnp.float32),
        (key_blocks, value_blocks, pos_blocks),
    )
    key_partial = key_parts.reshape(seq_total, local_kv * HD)
    value_partial = value_parts.reshape(seq_total, local_kv * HD)
    key_sum, value_sum = lax.psum((key_partial, value_partial), "ctx")
    first_row = lax.axis_index("ctx") * tok_rows
    key_sum = lax.dynamic_slice_in_dim(key_sum, first_row, tok_rows, 0)
    value_sum = lax.dynamic_slice_in_dim(value_sum, first_row, tok_rows, 0)
    query_low = grad_query.reshape(tok_rows, local_kv * QGROUP * HD).astype(jnp.bfloat16)
    regrouped = (
        lax.all_to_all(query_low, "head", split_axis=0, concat_axis=1, tiled=True),
        lax.all_to_all(
            key_sum.astype(jnp.bfloat16), "head", split_axis=0, concat_axis=1, tiled=True
        ),
        lax.all_to_all(
            value_sum.astype(jnp.bfloat16), "head", split_axis=0, concat_axis=1, tiled=True
        ),
    )
    return jnp.concatenate(regrouped, axis=1)


def solution(mesh):
    placed = (P("ctx", "head"), P("ctx", "head"), P("ctx", "head"), P("ctx", "head"), P())
    return jax.shard_map(
        shards, mesh=mesh, in_specs=placed, out_specs=P(("ctx", "head"), None), check_vma=False
    )
```

profile of v0, /device:TPU:2, one launch (start us, length us, event | category | flops | bytes accessed | tf_op | source)
XLA Modules:
  0.0 398.9 jit_solution(6545472219660576449)
XLA Ops:
  13.1 47.2 %all-gather.3.cloned.1.call-done = bf16[4096,128]{1,0:T(8,128)(2,1)} async-done(((bf16[128,128]{1,0:T(8,128)(2,1)}), bf16[4096,128]{1,0:T(8,128)(2,1)}) %all-gather.3.cloned.1.call-update) | async-done | bytes 1048592 | tf_op jit(solution)/shard_map/all_gather | solution.py:30
  60.4 16.3 %while.39 = (s32[]{:T(128)}, f32[1,8,128]{2,1,0:T(8,128)S(1)}, f32[1,8,128]{2,1,0:T(8,128)S(1)}, s32[8,512]{1,0:T(8,128)S(1)}, s32[128]{0:T(128)S(1)}, /*index=5...) while((s32[]{:T(128)}, f32[1,8,128]{2,1,0:T(8,128)S(1)}, ...), condition=%wide.region_5.6_spmd.clone, body=%wide.region_2.5_spmd.clone.sunk | while | flops 137958400 | bytes 4844652 | solution.py:63
  60.5 1.4 fusion.74
  62.6 1.4 fusion.74
  64.6 1.4 fusion.74
  66.6 1.4 fusion.74
  68.7 1.4 fusion.74
  70.7 1.4 fusion.74
  72.7 1.4 fusion.74
  74.8 1.4 fusion.74
  76.7 33.5 %all-gather.5.cloned.1.call-done = bf16[4096,128]{1,0:T(8,128)(2,1)} async-done(((bf16[128,128]{1,0:T(8,128)(2,1)}), bf16[4096,128]{1,0:T(8,128)(2,1)}) %all-gather.5.cloned.1.call-update) | async-done | bytes 1048592 | tf_op jit(solution)/shard_map/all_gather | solution.py:31
  110.1 25.6 %while.40 = (s32[]{:T(128)}, f32[1,8,128]{2,1,0:T(8,128)S(1)}, s32[8,512]{1,0:T(8,128)S(1)}, s32[128]{0:T(128)S(1)}, bf16[8,512,1,128]{3,1,2,0:T(8,128)(2,1)}, /...) while((s32[]{:T(128)}, f32[1,8,128]{2,1,0:T(8,128)S(1)}, ...), condition=%wide.region_8.9_spmd.clone, body=%wide.region_6.8_spmd.clone.sunk | while | flops 271123456 | bytes 5140091 | solution.py:81
  111.6 1.7 fusion.80
  113.3 1.3 fusion.79
  114.8 1.7 fusion.80
  118.0 1.7 fusion.80
  119.7 1.3 fusion.79
  121.2 1.7 fusion.80
  124.4 1.7 fusion.80
  126.1 1.3 fusion.79
  127.6 1.7 fusion.80
  130.8 1.7 fusion.80
  132.6 1.3 fusion.79
  134.1 1.7 fusion.80
  135.7 69.0 %while.41 = (s32[]{:T(128)}, f32[128,1,8,128]{0,3,2,1:T(8,128)}, f32[8,512,1,128]{3,1,2,0:T(8,128)}, f32[8,512,1,128]{3,1,2,0:T(8,128)}, bf16[8,512,1,128]{3,1,2...) while((s32[]{:T(128)}, f32[128,1,8,128]{0,3,2,1:T(8,128)}, ...), condition=%wide.region_10.11_spmd.clone, body=%wide.region_9.10_spmd.clone.sunk | while | flops 675610624 | bytes 12600467 | solution.py:103
  135.9 1.5 fusion.91
  137.4 1.5 fusion.92
  140.1 2.0 fusion.93
  142.1 2.1 fusion.95
  144.4 1.5 fusion.91
  145.9 1.5 fusion.92
  148.5 2.2 fusion.93
  150.8 2.1 fusion.95
  153.0 1.5 fusion.91
  154.5 1.5 fusion.92
  157.1 2.2 fusion.93
  159.4 2.1 fusion.95
  161.6 1.5 fusion.91
  163.2 1.5 fusion.92
  165.8 2.2 fusion.93
  168.0 2.1 fusion.95
  170.3 1.5 fusion.91
  171.8 1.5 fusion.92
  174.4 2.3 fusion.93
  176.7 2.1 fusion.95
  179.0 1.5 fusion.91
  180.5 1.5 fusion.92
  183.1 2.2 fusion.93
  185.4 2.1 fusion.95
  187.6 1.5 fusion.91
  189.1 1.5 fusion.92
  191.8 2.2 fusion.93
  194.0 2.1 fusion.95
  196.2 1.5 fusion.91
  197.7 1.5 fusion.92
  200.4 2.3 fusion.93
  202.6 2.1 fusion.95
  204.7 145.7 %all-reduce.2 = (bf16[4096,128]{1,0:T(8,128)(2,1)S(1)}, bf16[4096,128]{1,0:T(8,128)(2,1)S(1)}) all-reduce(f32[4096,128]{1,0:T(8,128)} %bitcast.8, f32[4096,128]{1,0:T(8,128)} %bitcast.5), channel_id=1, replica_groups=mesh['ctx'=32,'head'=8] {'ctx'}, use_global_device_ids=true, to_apply=%region_12.13 | all-reduce | flops 1048576 | bytes 6291456 | tf_op jit(solution)/shard_map/psum | solution.py:110
  351.1 7.0 %all-to-all-start.1 = ((bf16[8,16,128]{2,1,0:T(8,128)(2,1)}), bf16[8,16,128]{2,1,0:T(8,128)(2,1)S(1)}, u32[]{:S(2)}, u32[]{:S(2)}) async-start(bf16[8,16,128]{2,1,0:T(8,128)(2,1)} %bitcast.6), calls=%async_computation.1 | async-start | bytes 65536 | tf_op jit(solution)/shard_map/all_to_all | solution.py:117
  358.7 7.4 %all-to-all-done.1 = bf16[8,16,128]{2,1,0:T(8,128)(2,1)S(1)} async-done(((bf16[8,16,128]{2,1,0:T(8,128)(2,1)}), bf16[8,16,128]{2,1,0:T(8,128)(2,1)S(1)}, u32[]{:S(2)}, u32[]{:S(2)}) %all-to-all-start.1) | async-done | bytes 32800 | tf_op jit(solution)/shard_map/all_to_all | solution.py:117
  366.1 3.3 all-to-all-start.2
  370.5 7.0 %all-to-all-done.2 = bf16[8,16,128]{2,1,0:T(8,128)(2,1)S(1)} async-done(((bf16[8,16,128]{2,1,0:T(8,128)(2,1)}), bf16[8,16,128]{2,1,0:T(8,128)(2,1)S(1)}, u32[]{:S(2)}, u32[]{:S(2)}) %all-to-all-start.2) | async-done | bytes 32800 | tf_op jit(solution)/shard_map/all_to_all | solution.py:120
  377.5 3.4 all-to-all-start
  380.9 10.4 %all-to-all-done = bf16[8,16,1024]{2,1,0:T(8,128)(2,1)S(1)} async-done(((bf16[8,16,1024]{2,1,0:T(8,128)(2,1)}), bf16[8,16,1024]{2,1,0:T(8,128)(2,1)S(1)}, u32[]{:S(2)}, u32[]{:S(2)}) %all-to-all-start) | async-done | bytes 262176 | tf_op jit(solution)/shard_map/all_to_all | solution.py:116
  (134 shorter events, 31.3 us)
Async XLA Ops:
  6.5 53.8 %all-gather.3.cloned.1.call-start = ((), (), s32[]{:S(2)}) async-start(), calls=%async_computation.3 | async-start | bytes 1081344 | tf_op jit(solution)/shard_map/all_gather | solution.py:30
  7.3 102.9 %all-gather.5.cloned.1.call-start = ((), (), s32[]{:S(2)}) async-start(), calls=%async_computation.4 | async-start | bytes 1081344 | tf_op jit(solution)/shard_map/all_gather | solution.py:31
  204.7 164.7 %copy-start = (f32[128,1,8,128]{0,3,2,1:T(8,128)S(1)}, f32[128,1,8,128]{0,3,2,1:T(8,128)}, u32[]{:S(2)}) copy-start(f32[128,1,8,128]{0,3,2,1:T(8,128)} %get-tuple-element.157) | copy-start | bytes 1572868
  351.1 15.0 %all-to-all-start.1 = ((bf16[8,16,128]{2,1,0:T(8,128)(2,1)}), bf16[8,16,128]{2,1,0:T(8,128)(2,1)S(1)}, u32[]{:S(2)}, u32[]{:S(2)}) async-start(bf16[8,16,128]{2,1,0:T(8,128)(2,1)} %bitcast.6), calls=%async_computation.1 | async-start | bytes 65536 | tf_op jit(solution)/shard_map/all_to_all | solution.py:117
  366.1 11.4 %all-to-all-start.2 = ((bf16[8,16,128]{2,1,0:T(8,128)(2,1)}), bf16[8,16,128]{2,1,0:T(8,128)(2,1)S(1)}, u32[]{:S(2)}, u32[]{:S(2)}) async-start(bf16[8,16,128]{2,1,0:T(8,128)(2,1)} %bitcast.9), calls=%async_computation.2 | async-start | bytes 65536 | tf_op jit(solution)/shard_map/all_to_all | solution.py:120
  377.5 13.8 %all-to-all-start = ((bf16[8,16,1024]{2,1,0:T(8,128)(2,1)}), bf16[8,16,1024]{2,1,0:T(8,128)(2,1)S(1)}, u32[]{:S(2)}, u32[]{:S(2)}) async-start(bf16[8,16,1024]{2,1,0:T(8,128)(2,1)} %convert_element_type.20), calls=%async_computation | async-start | bytes 524288 | tf_op jit(solution)/shard_map/all_to_all | solution.py:116
Sparse Core Ops, SparseCore 0:
  9.9 50.4 all-gather.2
  62.9 47.1 all-gather.4
where the time goes:
time: 405 us; the launch traced here: 399 us
  blocking collectives  146 us (36%)
  waiting for transfers between devices  107 us (26%)
  matrix products  103 us (25%)
  starting transfers between devices  13.8 us (3%)
  between operations  13.6 us (3%)
  other arithmetic  9.49 us (2%)
  local copies, waits for them, and re-layouts  5.79 us (1%)
    psum x1, blocking collectives, shards(): key_sum, value_sum = lax.psum((key_partial, value_partial), 'ctx')  146 us
    all_gather x1, waiting for transfers between devices, shards(): lax.all_gather(keys, 'ctx', axis=0, tiled=True)  47.2 us
    dot_general x24, matrix products, scores(): jnp.einsum('igqd,jgd->gqij', query_heads, key_part, preferred_element_typ...  33.7 us
    all_gather x1, waiting for transfers between devices, shards(): lax.all_gather(values, 'ctx', axis=0, tiled=True)  33.5 us
    dot_general x16, matrix products, probs_and_grads(): jnp.einsum('igqd,jgd->gqij', grad_heads, value_part, preferred_element_ty...  25.1 us
    dot_general x8, matrix products, grad_step(): jnp.einsum('gqij,jgd->igqd', grad_score, key_part, preferred_element_type...  17.8 us
    dot_general x8, matrix products, grad_step(): jnp.einsum('gqij,igqd->jgd', probs_low, grad_heads, preferred_element_typ...  16.8 us
    all_to_all x1, waiting for transfers between devices, shards(): lax.all_to_all(query_low, 'head', split_axis=0, concat_axis=1, tiled=True)  10.4 us
  transfers between devices with their start and end apart: 5, of which 5 were waited for; matrix products, arithmetic and copies ran while one was open for 6% of the time, Pallas kernels for 0%

commit v1 on v0

v1 whole, which is shorter than its diff:
```python
import functools

import jax
import jax.numpy as jnp
from jax import lax
from jax.experimental import pallas as pl
from jax.experimental.pallas import tpu as pltpu
from jax.sharding import Mesh, PartitionSpec as P

HD = 128
QGROUP = 8
BLOCK = 64
NBLOCKS = 64
TOK = 128
CHIPS = 16
SEQ = 4096
TILE = 256
TILES = SEQ // TILE
ROWS = QGROUP * BLOCK
NEG = -1e30
SCALE = HD**-0.5
LOG2E = 1.4426950408889634


def mm(a, b):
    return jnp.dot(a, b, preferred_element_type=jnp.float32)


def fold(x, op):
    return op(x.reshape(x.shape[0] // 8, 8, x.shape[1]), axis=0)


def attention_kernel(
    order, place, q, g, own, other, dq, keep, send, ks, vs, kt, dk, dv, s_all, dp_all, qr, gr, qt, gt
):
    ctx = place[0]
    core = lax.rem(ctx, 2)
    chip_slots = [(i // 2) * 4 + i % 2 for i in range(2 * CHIPS)]

    def sorted_rows(i, half):
        start = order[chip_slots[i] + half * 2] * BLOCK
        return pl.ds(pl.multiple_of(start, BLOCK), BLOCK)

    for i in range(2 * CHIPS):
        rows = slice(i * BLOCK, (i + 1) * BLOCK)
        for src, half in ((own, core), (other, 1 - core)):
            dst = sorted_rows(i, half)
            ks[dst, :] = src[rows, :HD]
            vs[dst, :] = src[rows, HD:]

    def prepare(t, carry):
        rows = pl.ds(pl.multiple_of(t * TILE, TILE), TILE)
        kt[t] = ks[rows, :].T
        dk[t] = jnp.zeros((TILE, HD), jnp.float32)
        dv[t] = jnp.zeros((TILE, HD), jnp.float32)
        return carry

    lax.fori_loop(0, TILES, prepare, 0)

    for u in range(TOK // BLOCK):
        block = order[ctx * 2 + u]
        last = block // (TILE // BLOCK)
        for h in range(QGROUP):
            part = (slice(u * BLOCK, (u + 1) * BLOCK), slice(h * HD, (h + 1) * HD))
            qr[h * BLOCK : (h + 1) * BLOCK, :] = q[part]
            gr[h * BLOCK : (h + 1) * BLOCK, :] = g[part]
        qt[...] = qr[...].T
        gt[...] = gr[...].T

        def score(t):
            rows = pl.ds(pl.multiple_of(t * TILE, TILE), TILE)
            return mm(ks[rows, :], qt[...])

        def top_step(t, top):
            s = score(t)
            s_all[t] = s
            return jnp.maximum(top, fold(s, jnp.max))

        top = lax.fori_loop(0, last, top_step, jnp.full((8, ROWS), NEG, jnp.float32))
        s = score(last)
        key_pos = last * TILE + lax.broadcasted_iota(jnp.int32, s.shape, 0)
        row_pos = block * BLOCK + lax.rem(lax.broadcasted_iota(jnp.int32, s.shape, 1), BLOCK)
        s = jnp.where(key_pos <= row_pos, s, NEG)
        s_all[last] = s
        top = jnp.max(jnp.maximum(top, fold(s, jnp.max)), axis=0, keepdims=True)

        def sum_step(t, carry):
            total, delta = carry
            rows = pl.ds(pl.multiple_of(t * TILE, TILE), TILE)
            dp = mm(vs[rows, :], gt[...])
            p = jnp.exp2((s_all[t] - top) * (SCALE * LOG2E))
            s_all[t] = p
            dp_all[t] = dp
            return (total + fold(p, jnp.sum), delta + fold(p * dp, jnp.sum))

        zero = jnp.zeros((8, ROWS), jnp.float32)
        total, delta = lax.fori_loop(0, last + 1, sum_step, (zero, zero))
        inv = 1.0 / jnp.sum(total, axis=0, keepdims=True)
        delta = jnp.sum(delta, axis=0, keepdims=True) * inv

        def grad_step(t, dqt):
            p = s_all[t] * inv
            ds = (p * (dp_all[t] - delta) * SCALE).astype(jnp.bfloat16)
            dv[t] += mm(p.astype(jnp.bfloat16), gr[...])
            dk[t] += mm(ds, qr[...])
            return dqt + mm(kt[t], ds)

        dqt = lax.fori_loop(0, last + 1, grad_step, jnp.zeros((HD, ROWS), jnp.float32))
        out = dqt.T.astype(jnp.bfloat16)
        for h in range(QGROUP):
            part = (slice(u * BLOCK, (u + 1) * BLOCK), slice(h * HD, (h + 1) * HD))
            dq[part] = out[h * BLOCK : (h + 1) * BLOCK, :]

    for i in range(2 * CHIPS):
        rows = slice(i * BLOCK, (i + 1) * BLOCK)
        for dst, half in ((keep, core), (send, 1 - core)):
            block = order[chip_slots[i] + half * 2]
            tile = block // (TILE // BLOCK)
            src = pl.ds(pl.multiple_of(lax.rem(block, TILE // BLOCK) * BLOCK, BLOCK), BLOCK)
            dst[rows, :HD] = dk[tile, src, :].astype(jnp.bfloat16)
            dst[rows, HD:] = dv[tile, src, :].astype(jnp.bfloat16)


def attention(order, place, q, g, own, other):
    smem = pl.BlockSpec(memory_space=pltpu.SMEM)
    vmem = pl.BlockSpec(memory_space=pltpu.VMEM)
    half = CHIPS * TOK
    bf16, f32 = jnp.bfloat16, jnp.float32
    return pl.pallas_call(
        attention_kernel,
        out_shape=(
            jax.ShapeDtypeStruct((TOK, QGROUP * HD), bf16),
            jax.ShapeDtypeStruct((half, 2 * HD), bf16),
            jax.ShapeDtypeStruct((half, 2 * HD), bf16),
        ),
        in_specs=[smem, smem, vmem, vmem, vmem, vmem],
        out_specs=(vmem, vmem, vmem),
        scratch_shapes=[
            pltpu.VMEM((SEQ, HD), bf16),
            pltpu.VMEM((SEQ, HD), bf16),
            pltpu.VMEM((TILES, HD, TILE), bf16),
            pltpu.VMEM((TILES, TILE, HD), f32),
            pltpu.VMEM((TILES, TILE, HD), f32),
            pltpu.VMEM((TILES, TILE, ROWS), f32),
            pltpu.VMEM((TILES, TILE, ROWS), f32),
            pltpu.VMEM((ROWS, HD), bf16),
            pltpu.VMEM((ROWS, HD), bf16),
            pltpu.VMEM((HD, ROWS), bf16),
            pltpu.VMEM((HD, ROWS), bf16),
        ],
        compiler_params=pltpu.CompilerParams(vmem_limit_bytes=48 * 1024 * 1024),
        cost_estimate=pl.CostEstimate(
            flops=10 * TOK * QGROUP * SEQ * HD, bytes_accessed=6 * 1024 * 1024, transcendentals=TOK * QGROUP * SEQ
        ),
        name="attention",
    )(order, place, q, g, own, other)


def shards(queries, keys, values, out_grad, block_order):
    swap = [(0, 1), (1, 0)]
    plane = ("y", "x")
    kv = jnp.concatenate([keys, values], axis=1)
    spread = jnp.broadcast_to(kv[None], (CHIPS,) + kv.shape)
    own = lax.all_to_all(spread, plane, 0, 0, tiled=True).reshape(CHIPS * TOK, 2 * HD)
    other = lax.ppermute(own, "core", swap)
    place = lax.axis_index(("y", "x", "core")).astype(jnp.int32).reshape(1)
    dq, keep, send = attention(block_order, place, queries, out_grad, own, other)
    came = lax.ppermute(send, "core", swap)
    pair = (keep.astype(jnp.float32) + came.astype(jnp.float32)).astype(jnp.bfloat16)
    parts = lax.all_to_all(pair.reshape(CHIPS, TOK, 2 * HD), plane, 0, 0, tiled=True)
    dkv = jnp.sum(parts.astype(jnp.float32), axis=0).astype(jnp.bfloat16)
    mine = jnp.concatenate([dq, dkv], axis=1).reshape(8, TOK // 8, 10 * HD)
    got = lax.all_to_all(mine, "head", 0, 0, tiled=True).transpose(1, 0, 2)
    cols = [got[:, :, : 8 * HD], got[:, :, 8 * HD : 9 * HD], got[:, :, 9 * HD :]]
    return jnp.concatenate([c.reshape(TOK // 8, -1) for c in cols], axis=1)


def solution(mesh):
    split = Mesh(mesh.devices.reshape(4, 4, 2, 8), ("y", "x", "core", "head"))
    ctx = ("y", "x", "core")
    rows = P(ctx, "head")
    return jax.shard_map(
        shards,
        mesh=split,
        in_specs=(rows, rows, rows, rows, P()),
        out_specs=P(ctx + ("head",), None),
        check_vma=False,
    )
```

time: 405 us -> 97.4 us (0.24); the launches traced: 399 us -> 97.5 us
  matrix products: 103 us -> 0 us
  waiting for transfers between devices: 107 us -> 5.3 us
  blocking collectives: 146 us -> 73 us
  Pallas kernels: 0 us -> 16.8 us
  starting transfers between devices: 13.8 us -> 0.1 us
  between operations: 13.6 us -> 0.1 us
  other arithmetic: 9.49 us -> 1.98 us
  local copies, waits for them, and re-layouts: 5.79 us -> 0.17 us
    psum x1 -> x0, blocking collectives: 146 us -> none  [shards(): key_sum, value_sum = lax.psum((key_partial, value_partial), 'ctx')]
    dot_general x64 -> x0, matrix products: 103 us -> none  [the longest x24 33.7 us: scores(): jnp.einsum('igqd,jgd->gqij', query_heads, key_part, preferred_element_typ...]
    all_gather x2 -> x0, waiting for transfers between devices: 80.7 us -> none  [the longest x1 47.2 us: shards(): lax.all_gather(keys, 'ctx', axis=0, tiled=True)]
    all_to_all x0 -> x3, blocking collectives: none -> 73 us  [the longest x1 29.2 us: shards(): lax.all_to_all(pair.reshape(CHIPS, TOK, 2 * HD), plane, 0, 0, tiled=True)]
    all_to_all x3 -> x0, waiting for transfers between devices: 24.7 us -> none  [the longest x1 10.4 us: shards(): lax.all_to_all(query_low, 'head', split_axis=0, concat_axis=1, tiled=True)]
    pallas_call x0 -> x1, Pallas kernels: none -> 16.8 us  [attention(): pl.pallas_call(attention_kernel, out_shape=(jax.ShapeDtypeStruct((TOK, QG...]
    all_to_all x3 -> x0, starting transfers between devices: 13.8 us -> none  [the longest x1 7.01 us: shards(): lax.all_to_all(key_sum.astype(jnp.bfloat16), 'head', split_axis=0, concat...]
    ppermute x0 -> x2, waiting for transfers between devices: none -> 5.3 us  [the longest x1 2.66 us: shards(): other = lax.ppermute(own, 'core', swap)]
  transfers between devices with their start and end apart: 5 -> 2, of which waited for: 5 -> 2; matrix products, arithmetic and copies ran while one was open for 6% -> 0% of each run, Pallas kernels for 0% -> 0%
where the time goes in v1:
time: 97.4 us; the launch traced here: 97.5 us
  blocking collectives  73 us (75%)
  Pallas kernels  16.8 us (17%)
  waiting for transfers between devices  5.3 us (5%)
  other arithmetic  1.98 us (2%)
    all_to_all x1, blocking collectives, shards(): lax.all_to_all(pair.reshape(CHIPS, TOK, 2 * HD), plane, 0, 0, tiled=True)  29.2 us
    all_to_all x1, blocking collectives, shards(): lax.all_to_all(spread, plane, 0, 0, tiled=True).reshape(CHIPS * TOK, 2 * HD)  23.2 us
    all_to_all x1, blocking collectives, shards(): got = lax.all_to_all(mine, 'head', 0, 0, tiled=True).transpose(1, 0, 2)  20.6 us
    pallas_call x1, Pallas kernels, attention(): pl.pallas_call(attention_kernel, out_shape=(jax.ShapeDtypeStruct((TOK, QG...  16.8 us
    ppermute x1, waiting for transfers between devices, shards(): other = lax.ppermute(own, 'core', swap)  2.66 us
    ppermute x1, waiting for transfers between devices, shards(): came = lax.ppermute(send, 'core', swap)  2.65 us
  transfers between devices with their start and end apart: 2, of which 2 were waited for; matrix products, arithmetic and copies ran while one was open for 0% of the time, Pallas kernels for 0%

profile of v1, /device:TPU:2, one launch (start us, length us, event | category | flops | bytes accessed | tf_op | source)
XLA Modules:
  0.0 97.5 jit_solution(10455555833256891725)
XLA Ops:
  0.0 0.8 pad_maximum_fusion.2
  0.8 0.1 broadcast_in_dim.2
  0.9 0.0 copy-start
  0.9 0.0 copy-start.1
  0.9 0.0 copy-start.2
  0.9 23.2 %all_to_all.15 = bf16[16,128,256]{2,1,0:T(8,128)(2,1)S(1)} all-to-all(bf16[16,128,256]{2,1,0:T(8,128)(2,1)S(1)} %broadcast_in_dim.2), channel_id=1, replica_groups=mesh['y'=4,'x'=4,'core'=2,'head'=8] {'y','x'}, dimensions={0} | all-to-all | bytes 2097152 | tf_op jit(solution)/shard_map/all_to_all | solution.py:164
  24.1 0.0 collective-permute-start
  24.1 2.7 %collective-permute-done.other = bf16[2048,256]{1,0:T(8,128)(2,1)S(1)} collective-permute-done((bf16[2048,256]{1,0:T(8,128)(2,1)S(1)}, bf16[2048,256]{1,0:T(8,128)(2,1)S(1)}, u32[]{:S(2)}, u32[]{:S(2)}) %collective-permute-start) | collective-permute-done | bytes 1048608 | tf_op jit(solution)/shard_map/ppermute | solution.py:165
  26.8 0.0 copy-done
  26.8 0.0 copy-done.1
  26.8 0.0 copy-done.2
  26.8 16.8 %attention.1 = (bf16[128,1024]{1,0:T(8,128)(2,1)S(1)}, bf16[2048,256]{1,0:T(8,128)(2,1)S(1)}, bf16[2048,256]{1,0:T(8,128)(2,1)S(1)}) custom-call(s32[64]{0:T(128)S(1)} %copy-done.2, s32[1]{0:T(128)} %bitcast.place, bf16[128,1024]{1,0:T(8,128)(2,1)S(1)} %copy-done, bf16[128,1024]{1,0:T(8,128)(2,1)S(1)} %copy-done.1, bf16[2048,256]{1,0:T(8,128)(2,1)S(1)} %bitcast.17, ...), custom_call_target="tpu_custom_call" | custom-call | flops 5368709120 | bytes 6291456 | tf_op jit(solution)/shard_map/attention/pallas_call | solution.py:129
  43.6 0.1 collective-permute-start.1
  43.7 2.6 %collective-permute-done.1 = bf16[2048,256]{1,0:T(8,128)(2,1)S(1)} collective-permute-done((bf16[2048,256]{1,0:T(8,128)(2,1)S(1)}, bf16[2048,256]{1,0:T(8,128)(2,1)S(1)}, u32[]{:S(2)}, u32[]{:S(2)}) %collective-permute-start.1) | collective-permute-done | bytes 1048608 | tf_op jit(solution)/shard_map/ppermute | solution.py:168
  46.4 0.3 add_convert_fusion
  46.6 29.2 %all_to_all.16 = bf16[16,128,256]{2,1,0:T(8,128)(2,1)S(1)} all-to-all(bf16[16,128,256]{2,1,0:T(8,128)(2,1)S(1)} %bitcast.18), channel_id=1, replica_groups=mesh['y'=4,'x'=4,'core'=2,'head'=8] {'y','x'}, dimensions={0} | all-to-all | bytes 2097152 | tf_op jit(solution)/shard_map/all_to_all | solution.py:170
  75.9 0.1 reduce_sum.12
  76.1 20.6 %all_to_all.17 = bf16[8,16,1280]{2,1,0:T(8,128)(2,1)S(1)} all-to-all(bf16[8,16,1280]{2,1,0:T(8,128)(2,1)S(1)} %bitcast.21), channel_id=1, replica_groups=mesh['y'=4,'x'=4,'core'=2,'head'=8] {'head'}, dimensions={0} | all-to-all | bytes 655360 | tf_op jit(solution)/shard_map/all_to_all | solution.py:173
  96.7 0.7 pad_maximum_fusion.1
  (5 shorter events, 0.1 us)
Async XLA Ops:
  0.9 25.9 %copy-start = (bf16[128,1024]{1,0:T(8,128)(2,1)S(1)}, bf16[128,1024]{1,0:T(8,128)(2,1)}, u32[]{:S(2)}) copy-start(bf16[128,1024]{1,0:T(8,128)(2,1)} %q.1) | copy-start | bytes 786436
  0.9 25.9 %copy-start.1 = (bf16[128,1024]{1,0:T(8,128)(2,1)S(1)}, bf16[128,1024]{1,0:T(8,128)(2,1)}, u32[]{:S(2)}) copy-start(bf16[128,1024]{1,0:T(8,128)(2,1)} %g.1) | copy-start | bytes 786436
  0.9 25.9 %copy-start.2 = (s32[64]{0:T(128)S(1)}, s32[64]{0:T(128)}, u32[]{:S(2)}) copy-start(s32[64]{0:T(128)} %order.1) | copy-start | bytes 772
  24.1 2.7 %collective-permute-start = (bf16[2048,256]{1,0:T(8,128)(2,1)S(1)}, bf16[2048,256]{1,0:T(8,128)(2,1)S(1)}, u32[]{:S(2)}, u32[]{:S(2)}) collective-permute-start(bf16[2048,256]{1,0:T(8,128)(2,1)S(1)} %bitcast.16), channel_id=1, source_target_pairs={{0,8},{8,0},{1,9},{9,1},{2,10},{10,2},{3,11},{11,3},{4,12},{12,4},... | collective-permute-start | bytes 3145736 | tf_op jit(solution)/shard_map/ppermute | solution.py:165
  43.6 2.7 %collective-permute-start.1 = (bf16[2048,256]{1,0:T(8,128)(2,1)S(1)}, bf16[2048,256]{1,0:T(8,128)(2,1)S(1)}, u32[]{:S(2)}, u32[]{:S(2)}) collective-permute-start(bf16[2048,256]{1,0:T(8,128)(2,1)S(1)} %get-tuple-element.10), channel_id=1, source_target_pairs={{0,8},{8,0},{1,9},{9,1},{2,10},{10,2},{3,11},{11,3},{4,12},{12,4},... | collective-permute-start | bytes 3145736 | tf_op jit(solution)/shard_map/ppermute | solution.py:168

commit v2 on v1

v2 whole, which is shorter than its diff:
```python
import jax
import jax.numpy as jnp
from jax import lax
from jax.experimental import pallas as pl
from jax.experimental.pallas import tpu as pltpu
from jax.sharding import Mesh, PartitionSpec as P

HD = 128
QGROUP = 8
BLOCK = 64
TOK = 128
CHIPS = 16
HALF = CHIPS * TOK
OWN_BLOCKS = HALF // BLOCK
UNITS = 4
TILE = 256
STEP = 1024
ROWS = QGROUP * BLOCK
NEG = -1e30
SCALE = HD**-0.5
LOG2E = 1.4426950408889634
BF16 = jnp.bfloat16
F32 = jnp.float32


def mm(a, b):
    return jnp.dot(a, b, preferred_element_type=F32)


def fold(x, op):
    return op(x.reshape(x.shape[0] // 8, 8, x.shape[1]), axis=0)


def step_rows(i):
    return pl.ds(pl.multiple_of(i * STEP, STEP), STEP)


def block_rows(i):
    return pl.ds(pl.multiple_of(i * BLOCK, BLOCK), BLOCK)


def unit_rows(u):
    return pl.ds(pl.multiple_of(u * ROWS, ROWS), ROWS)


def stats_kernel(
    order, place, q_own, q_other, g_own, g_other, kv,
    stats, p_all, dp_all, kt, qr, gr, rank, held,
    ks, vs, qt, gt, owner, upto,
):
    ctx = place[0]
    core = lax.rem(ctx, 2)

    def clear(p, carry):
        owner[p] = -1
        return carry

    lax.fori_loop(0, 2 * OWN_BLOCKS, clear, 0, unroll=True)
    for i in range(OWN_BLOCKS):
        owner[order[(i // 2) * 4 + core * 2 + i % 2]] = i

    def count(p, seen):
        i = owner[p]
        mine = i >= 0

        @pl.when(mine)
        def _():
            rank[i] = seen

        seen = seen + mine.astype(jnp.int32)
        upto[p] = seen
        return seen

    lax.fori_loop(0, 2 * OWN_BLOCKS, count, 0)

    for i in range(OWN_BLOCKS):
        rows = slice(i * BLOCK, (i + 1) * BLOCK)
        dst = block_rows(rank[i])
        ks[dst, :] = kv[rows, :HD]
        vs[dst, :] = kv[rows, HD:]
    for j in range(HALF // TILE):
        kt[j] = ks[j * TILE : (j + 1) * TILE, :].T
    for u in range(UNITS):
        q, g = ((q_own, g_own), (q_other, g_other))[u // 2]
        for h in range(QGROUP):
            part = (slice(u % 2 * BLOCK, (u % 2 + 1) * BLOCK), slice(h * HD, (h + 1) * HD))
            rows = slice(u * ROWS + h * BLOCK, u * ROWS + (h + 1) * BLOCK)
            qr[rows, :] = q[part]
            gr[rows, :] = g[part]

    def unit(u, carry):
        slot = (ctx + (u // 2) * (1 - 2 * core)) * 2 + lax.rem(u, 2)
        block = order[slot]
        seen = upto[block]
        held[u] = seen
        steps = (seen * BLOCK + STEP - 1) // STEP
        diagonal = owner[block] >= 0
        lane = lax.rem(lax.broadcasted_iota(jnp.int32, (1, ROWS), 1), BLOCK)
        limit = (seen - 1) * BLOCK + jnp.where(diagonal, lane, BLOCK - 1)
        qt[...] = qr[unit_rows(u), :].T
        gt[...] = gr[unit_rows(u), :].T

        def top_step(i, top):
            s = mm(ks[step_rows(i), :], qt[...])
            key = lax.broadcasted_iota(jnp.int32, s.shape, 0)
            s = jnp.where(key <= limit - i * STEP, s, NEG)
            p_all[u, step_rows(i), :] = s
            return jnp.maximum(top, fold(s, jnp.max))

        top = lax.fori_loop(0, steps, top_step, jnp.full((8, ROWS), NEG, F32))
        top = jnp.max(top, axis=0, keepdims=True)

        def sum_step(i, carry):
            total, delta = carry
            rows = step_rows(i)
            dp = mm(vs[rows, :], gt[...])
            p = jnp.exp2((p_all[u, rows, :] - top) * (SCALE * LOG2E))
            p_all[u, rows, :] = p
            dp_all[u, rows, :] = dp
            return (total + fold(p, jnp.sum), delta + fold(p * dp, jnp.sum))

        zero = jnp.zeros((8, ROWS), F32)
        total, delta = lax.fori_loop(0, steps, sum_step, (zero, zero))
        stats[u, 0:1, :] = top
        stats[u, 1:2, :] = jnp.sum(total, axis=0, keepdims=True)
        stats[u, 2:3, :] = jnp.sum(delta, axis=0, keepdims=True)
        stats[u, 3:8, :] = jnp.zeros((5, ROWS), F32)
        return carry

    lax.fori_loop(0, UNITS, unit, 0)


def grads_kernel(
    rank, held, stats, came, p_all, dp_all, kt, qr, gr,
    dq_own, dq_other, dkv,
    dk, dv, dqt,
):
    dk[...] = jnp.zeros((HALF, HD), F32)
    dv[...] = jnp.zeros((HALF, HD), F32)
    dqt[...] = jnp.zeros((UNITS, HD, ROWS), F32)

    def unit(u, carry):
        other = lax.rem(u + 2, UNITS)
        steps = (held[u] * BLOCK + STEP - 1) // STEP
        top, total, delta = (stats[u, k : k + 1, :] for k in range(3))
        top2, total2, delta2 = (came[other, k : k + 1, :] for k in range(3))
        both = jnp.maximum(top, top2)
        w = jnp.exp2((top - both) * (SCALE * LOG2E))
        w2 = jnp.exp2((top2 - both) * (SCALE * LOG2E))
        inv = 1.0 / (total * w + total2 * w2)
        delta = (delta * w + delta2 * w2) * inv
        w = w * inv

        def grad_step(i, carry):
            rows = step_rows(i)
            p = p_all[u, rows, :] * w
            ds = (p * (dp_all[u, rows, :] - delta) * SCALE).astype(BF16)
            dv[rows, :] += mm(p.astype(BF16), gr[unit_rows(u), :])
            dk[rows, :] += mm(ds, qr[unit_rows(u), :])
            part = mm(kt[i * (STEP // TILE)], ds[:TILE])
            for j in range(1, STEP // TILE):
                part += mm(kt[i * (STEP // TILE) + j], ds[j * TILE : (j + 1) * TILE])
            dqt[u] += part
            return carry

        lax.fori_loop(0, steps, grad_step, 0)
        return carry

    lax.fori_loop(0, UNITS, unit, 0)
    for u in range(UNITS):
        dq = (dq_own, dq_other)[u // 2]
        out = dqt[u].T
        for h in range(QGROUP):
            part = (slice(u % 2 * BLOCK, (u % 2 + 1) * BLOCK), slice(h * HD, (h + 1) * HD))
            dq[part] = out[h * BLOCK : (h + 1) * BLOCK, :]
    for i in range(OWN_BLOCKS):
        rows = slice(i * BLOCK, (i + 1) * BLOCK)
        src = block_rows(rank[i])
        dkv[rows, :HD] = dk[src, :].astype(BF16)
        dkv[rows, HD:] = dv[src, :].astype(BF16)


def attention(order, place, q_own, q_other, g_own, g_other, kv, swap):
    smem = pl.BlockSpec(memory_space=pltpu.SMEM)
    vmem = pl.BlockSpec(memory_space=pltpu.VMEM)
    shape = jax.ShapeDtypeStruct
    params = pltpu.CompilerParams(vmem_limit_bytes=10 * 1024 * 1024)
    pairs = UNITS * ROWS * HALF
    stats, p_all, dp_all, kt, qr, gr, rank, held = pl.pallas_call(
        stats_kernel,
        out_shape=(
            shape((UNITS, 8, ROWS), F32),
            shape((UNITS, HALF, ROWS), F32),
            shape((UNITS, HALF, ROWS), F32),
            shape((HALF // TILE, HD, TILE), BF16),
            shape((UNITS * ROWS, HD), BF16),
            shape((UNITS * ROWS, HD), BF16),
            shape((OWN_BLOCKS,), jnp.int32),
            shape((UNITS,), jnp.int32),
        ),
        in_specs=[smem, smem] + [vmem] * 5,
        out_specs=(vmem,) * 6 + (smem, smem),
        scratch_shapes=[
            pltpu.VMEM((HALF, HD), BF16),
            pltpu.VMEM((HALF, HD), BF16),
            pltpu.VMEM((HD, ROWS), BF16),
            pltpu.VMEM((HD, ROWS), BF16),
            pltpu.SMEM((2 * OWN_BLOCKS,), jnp.int32),
            pltpu.SMEM((2 * OWN_BLOCKS,), jnp.int32),
        ],
        compiler_params=params,
        cost_estimate=pl.CostEstimate(flops=4 * pairs * HD, bytes_accessed=4 * 2**20, transcendentals=pairs),
        name="stats",
    )(order, place, q_own, q_other, g_own, g_other, kv)
    came = swap(stats)
    return pl.pallas_call(
        grads_kernel,
        out_shape=(
            shape((TOK, QGROUP * HD), F32),
            shape((TOK, QGROUP * HD), F32),
            shape((HALF, 2 * HD), BF16),
        ),
        in_specs=[smem, smem] + [vmem] * 7,
        out_specs=(vmem,) * 3,
        scratch_shapes=[
            pltpu.VMEM((HALF, HD), F32),
            pltpu.VMEM((HALF, HD), F32),
            pltpu.VMEM((UNITS, HD, ROWS), F32),
        ],
        compiler_params=params,
        cost_estimate=pl.CostEstimate(flops=6 * pairs * HD, bytes_accessed=4 * 2**20, transcendentals=0),
        name="grads",
    )(rank, held, stats, came, p_all, dp_all, kt, qr, gr)


def shards(queries, keys, values, out_grad, block_order):
    plane = ("y", "x")

    def swap(x):
        return lax.ppermute(x, "core", [(0, 1), (1, 0)])

    q_other, g_other = swap(queries), swap(out_grad)
    kv = jnp.concatenate([keys, values], axis=1)
    spread = jnp.broadcast_to(kv[None], (CHIPS,) + kv.shape)
    gathered = lax.all_to_all(spread, plane, 0, 0, tiled=True).reshape(HALF, 2 * HD)
    place = lax.axis_index(("y", "x", "core")).astype(jnp.int32).reshape(1)
    dq_own, dq_other, dkv = attention(
        block_order, place, queries, q_other, out_grad, g_other, gathered, swap
    )
    dq_came = swap(dq_other)
    parts = lax.all_to_all(dkv.reshape(CHIPS, TOK, 2 * HD), plane, 0, 0, tiled=True)
    dkv = jnp.sum(parts.astype(F32), axis=0).astype(BF16)
    dq = (dq_own + dq_came).astype(BF16)
    mine = jnp.concatenate([dq, dkv], axis=1).reshape(8, TOK // 8, 10 * HD)
    got = lax.all_to_all(mine, "head", 0, 0, tiled=True).transpose(1, 0, 2)
    cols = [got[:, :, : 8 * HD], got[:, :, 8 * HD : 9 * HD], got[:, :, 9 * HD :]]
    return jnp.concatenate([c.reshape(TOK // 8, -1) for c in cols], axis=1)


def solution(mesh):
    split = Mesh(mesh.devices.reshape(4, 4, 2, 8), ("y", "x", "core", "head"))
    ctx = ("y", "x", "core")
    rows = P(ctx, "head")
    return jax.shard_map(
        shards,
        mesh=split,
        in_specs=(rows, rows, rows, rows, P()),
        out_specs=P(ctx + ("head",), None),
        check_vma=False,
    )
```

time: 97.4 us -> 90.5 us (0.929); the launches traced: 97.5 us -> 89.3 us
  blocking collectives: 73 us -> 19.6 us
  waiting for transfers between devices: 5.3 us -> 31.6 us
  starting transfers between devices: 0.1 us -> 14.4 us
  local copies, waits for them, and re-layouts: 0.17 us -> 3.69 us
  Pallas kernels: 16.8 us -> 18.1 us
    all_to_all x2 -> x0, blocking collectives: 52.4 us -> none  [the longest x1 29.2 us: shards(): lax.all_to_all(pair.reshape(CHIPS, TOK, 2 * HD), plane, 0, 0, tiled=True)]
    all_to_all x0 -> x2, waiting for transfers between devices: none -> 26.9 us  [the longest x1 13.7 us: shards(): lax.all_to_all(spread, plane, 0, 0, tiled=True).reshape(HALF, 2 * HD)]
    all_to_all x0 -> x2, starting transfers between devices: none -> 13.8 us  [the longest x1 7.48 us: shards(): lax.all_to_all(spread, plane, 0, 0, tiled=True).reshape(HALF, 2 * HD)]
    unnamed x8, local copies, waits for them, and re-layouts: 0.05 us -> 2.59 us
    pallas_call x1 -> x2, Pallas kernels: 16.8 us -> 18.1 us  [the longest x1 9.3 us: attention(): pl.pallas_call(stats_kernel, out_shape=(shape((UNITS, 8, ROWS), F32), sha...]
    all_to_all x1, blocking collectives: 20.6 us -> 19.6 us  [shards(): got = lax.all_to_all(mine, 'head', 0, 0, tiled=True).transpose(1, 0, 2)]
    broadcast_in_dim x1, local copies, waits for them, and re-layouts: 0.09 us -> 1.08 us  [shards(): spread = jnp.broadcast_to(kv[None], (CHIPS,) + kv.shape)]
    ppermute x2 -> x4, waiting for transfers between devices: 5.3 us -> 4.75 us  [swap(): return lax.ppermute(x, 'core', [(0, 1), (1, 0)])]
  transfers between devices with their start and end apart: 2 -> 6, of which waited for: 2 -> 6; matrix products, arithmetic and copies ran while one was open for 0% -> 0% of each run, Pallas kernels for 0% -> 0%
where the time goes in v2:
time: 90.5 us; the launch traced here: 89.3 us
  waiting for transfers between devices  31.6 us (35%)
  blocking collectives  19.6 us (22%)
  Pallas kernels  18.1 us (20%)
  starting transfers between devices  14.4 us (16%)
  local copies, waits for them, and re-layouts  3.69 us (4%)
  other arithmetic  1.77 us (2%)
    all_to_all x1, blocking collectives, shards(): got = lax.all_to_all(mine, 'head', 0, 0, tiled=True).transpose(1, 0, 2)  19.6 us
    all_to_all x1, waiting for transfers between devices, shards(): lax.all_to_all(spread, plane, 0, 0, tiled=True).reshape(HALF, 2 * HD)  13.7 us
    all_to_all x1, waiting for transfers between devices, shards(): lax.all_to_all(dkv.reshape(CHIPS, TOK, 2 * HD), plane, 0, 0, tiled=True)  13.2 us
    pallas_call x1, Pallas kernels, attention(): pl.pallas_call(stats_kernel, out_shape=(shape((UNITS, 8, ROWS), F32), sha...  9.3 us
    pallas_call x1, Pallas kernels, attention(): pl.pallas_call(grads_kernel, out_shape=(shape((TOK, QGROUP * HD), F32), s...  8.83 us
    all_to_all x1, starting transfers between devices, shards(): lax.all_to_all(spread, plane, 0, 0, tiled=True).reshape(HALF, 2 * HD)  7.48 us
    all_to_all x1, starting transfers between devices, shards(): lax.all_to_all(dkv.reshape(CHIPS, TOK, 2 * HD), plane, 0, 0, tiled=True)  6.34 us
    ppermute x4, waiting for transfers between devices, swap(): return lax.ppermute(x, 'core', [(0, 1), (1, 0)])  4.75 us
  transfers between devices with their start and end apart: 6, of which 6 were waited for; matrix products, arithmetic and copies ran while one was open for 0% of the time, Pallas kernels for 0%

profile of v2, /device:TPU:2, one launch (start us, length us, event | category | flops | bytes accessed | tf_op | source)
XLA Modules:
  0.0 89.3 jit_solution(5856199872274964436)
XLA Ops:
  0.0 0.8 pad_maximum_fusion.2
  0.8 1.1 %broadcast_in_dim.2 = bf16[16,128,256]{2,1,0:T(8,128)(2,1)} broadcast(bf16[128,256]{1,0:T(8,128)(2,1)S(1)} %pad_maximum_fusion.2), dimensions={1,2} | broadcast | bytes 1114112 | tf_op jit(solution)/shard_map/broadcast_in_dim | solution.py:244
  1.9 7.5 %all-to-all-start = ((bf16[16,128,256]{2,1,0:T(8,128)(2,1)}), bf16[16,128,256]{2,1,0:T(8,128)(2,1)S(1)}, u32[]{:S(2)}, u32[]{:S(2)}) async-start(bf16[16,128,256]{2,1,0:T(8,128)(2,1)} %broadcast_in_dim.2), calls=%async_computation | async-start | bytes 2097152 | tf_op jit(solution)/shard_map/all_to_all | solution.py:245
  9.3 0.0 collective-permute-start
  9.3 0.5 collective-permute-start.1
  9.8 1.2 %collective-permute-done.q_other = bf16[128,1024]{1,0:T(8,128)(2,1)S(1)} collective-permute-done((bf16[128,1024]{1,0:T(8,128)(2,1)}, bf16[128,1024]{1,0:T(8,128)(2,1)S(1)}, u32[]{:S(2)}, u32[]{:S(2)}) %collective-permute-start) | collective-permute-done | bytes 262176 | tf_op jit(solution)/shard_map/ppermute | solution.py:240
  11.1 0.4 collective-permute-done.1.g_other
  11.5 13.7 %all-to-all-done = bf16[16,128,256]{2,1,0:T(8,128)(2,1)S(1)} async-done(((bf16[16,128,256]{2,1,0:T(8,128)(2,1)}), bf16[16,128,256]{2,1,0:T(8,128)(2,1)S(1)}, u32[]{:S(2)}, u32[]{:S(2)}) %all-to-all-start) | async-done | bytes 1048608 | tf_op jit(solution)/shard_map/all_to_all | solution.py:245
  25.1 0.0 copy-start
  25.1 0.9 %copy-done = bf16[128,1024]{1,0:T(8,128)(2,1)S(1)} copy-done((bf16[128,1024]{1,0:T(8,128)(2,1)S(1)}, bf16[128,1024]{1,0:T(8,128)(2,1)}, u32[]{:S(2)}) %copy-start) | copy-done | bytes 262168
  26.1 0.0 copy-start.1
  26.1 0.9 %copy-done.1 = bf16[128,1024]{1,0:T(8,128)(2,1)S(1)} copy-done((bf16[128,1024]{1,0:T(8,128)(2,1)S(1)}, bf16[128,1024]{1,0:T(8,128)(2,1)}, u32[]{:S(2)}) %copy-start.1) | copy-done | bytes 262168
  27.0 0.0 copy-start.2
  27.0 0.7 copy-done.2
  27.7 9.3 %stats.1 = (f32[4,8,512]{2,1,0:T(8,128)S(1)}, f32[4,2048,512]{2,1,0:T(8,128)S(1)}, f32[4,2048,512]{2,1,0:T(8,128)S(1)}, bf16[8,128,256]{2,1,0:T(8,128)(2,1)S(1)}...) custom-call(s32[64]{0:T(128)S(1)} %copy-done.2, s32[1]{0:T(128)} %bitcast.place, ...), custom_call_target="tpu_custom_call" | custom-call | flops 2147483648 | bytes 4194304 | tf_op jit(solution)/shard_map/stats/pallas_call | solution.py:189
  37.0 0.1 collective-permute-start.2
  37.1 1.2 %collective-permute-done.2.came = f32[4,8,512]{2,1,0:T(8,128)S(1)} collective-permute-done((f32[4,8,512]{2,1,0:T(8,128)S(1)}, f32[4,8,512]{2,1,0:T(8,128)S(1)}, u32[]{:S(2)}, u32[]{:S(2)}) %collective-permute-start.2) | collective-permute-done | bytes 65568 | tf_op jit(solution)/shard_map/ppermute | solution.py:240
  38.3 8.8 %grads.1 = (f32[128,1024]{1,0:T(8,128)S(1)}, f32[128,1024]{1,0:T(8,128)S(1)}, bf16[2048,256]{1,0:T(8,128)(2,1)}) custom-call(s32[32]{0:T(128)S(1)} %get-tuple-element.16.rank, s32[4]{0:T(128)S(1)} %get-tuple-element.17.held, f32[4,8,512]{2,1,0:T(8,128)S(1)} %get-tuple-element.18.stats, f32[4,8,512]{2,1,0:T(8,128)S(1)} %collective-permute-done.2.came, ...), custom_call_target="tpu_custom_call" | custom-call | flops 3221225472 | bytes 4194304 | tf_op jit(solution)/shard_map/grads/pallas_call | solution.py:216
  47.2 6.3 %all-to-all-start.1 = ((bf16[16,128,256]{2,1,0:T(8,128)(2,1)}), bf16[16,128,256]{2,1,0:T(8,128)(2,1)S(1)}, u32[]{:S(2)}, u32[]{:S(2)}) async-start(bf16[16,128,256]{2,1,0:T(8,128)(2,1)} %bitcast.2), calls=%async_computation.1 | async-start | bytes 2097152 | tf_op jit(solution)/shard_map/all_to_all | solution.py:251
  53.5 0.0 collective-permute-start.3
  53.5 1.9 %collective-permute-done.3 = f32[128,1024]{1,0:T(8,128)S(1)} collective-permute-done((f32[128,1024]{1,0:T(8,128)S(1)}, f32[128,1024]{1,0:T(8,128)S(1)}, u32[]{:S(2)}, u32[]{:S(2)}) %collective-permute-start.3) | collective-permute-done | bytes 524320 | tf_op jit(solution)/shard_map/ppermute | solution.py:240
  55.4 0.1 add_convert_fusion
  55.5 13.2 %all-to-all-done.1 = bf16[16,128,256]{2,1,0:T(8,128)(2,1)S(1)} async-done(((bf16[16,128,256]{2,1,0:T(8,128)(2,1)}), bf16[16,128,256]{2,1,0:T(8,128)(2,1)S(1)}, u32[]{:S(2)}, u32[]{:S(2)}) %all-to-all-start.1) | async-done | bytes 1048608 | tf_op jit(solution)/shard_map/all_to_all | solution.py:251
  68.7 0.1 reduce_sum.12
  68.9 19.6 %all_to_all.15 = bf16[8,16,1280]{2,1,0:T(8,128)(2,1)S(1)} all-to-all(bf16[8,16,1280]{2,1,0:T(8,128)(2,1)S(1)} %bitcast.19), channel_id=1, replica_groups=mesh['y'=4,'x'=4,'core'=2,'head'=8] {'head'}, dimensions={0} | all-to-all | bytes 655360 | tf_op jit(solution)/shard_map/all_to_all | solution.py:255
  88.5 0.7 pad_maximum_fusion.1
  (5 shorter events, 0.1 us)
Async XLA Ops:
  1.9 23.3 %all-to-all-start = ((bf16[16,128,256]{2,1,0:T(8,128)(2,1)}), bf16[16,128,256]{2,1,0:T(8,128)(2,1)S(1)}, u32[]{:S(2)}, u32[]{:S(2)}) async-start(bf16[16,128,256]{2,1,0:T(8,128)(2,1)} %broadcast_in_dim.2), calls=%async_computation | async-start | bytes 2097152 | tf_op jit(solution)/shard_map/all_to_all | solution.py:245
  9.3 1.7 %collective-permute-start = (bf16[128,1024]{1,0:T(8,128)(2,1)}, bf16[128,1024]{1,0:T(8,128)(2,1)S(1)}, u32[]{:S(2)}, u32[]{:S(2)}) collective-permute-start(bf16[128,1024]{1,0:T(8,128)(2,1)} %q_own.1), channel_id=1, source_target_pairs={{0,8},{8,0},{1,9},{9,1},{2,10},{10,2},{3,11},{11,3},{4,12},{12,4},... | collective-permute-start | bytes 786440 | tf_op jit(solution)/shard_map/ppermute | solution.py:240
  9.3 2.1 %collective-permute-start.1 = (bf16[128,1024]{1,0:T(8,128)(2,1)}, bf16[128,1024]{1,0:T(8,128)(2,1)S(1)}, u32[]{:S(2)}, u32[]{:S(2)}) collective-permute-start(bf16[128,1024]{1,0:T(8,128)(2,1)} %g_own.1), channel_id=1, source_target_pairs={{0,8},{8,0},{1,9},{9,1},{2,10},{10,2},{3,11},{11,3},{4,12},{12,4},... | collective-permute-start | bytes 786440 | tf_op jit(solution)/shard_map/ppermute | solution.py:240
  25.1 1.0 %copy-start = (bf16[128,1024]{1,0:T(8,128)(2,1)S(1)}, bf16[128,1024]{1,0:T(8,128)(2,1)}, u32[]{:S(2)}) copy-start(bf16[128,1024]{1,0:T(8,128)(2,1)} %q_own.1) | copy-start | bytes 786436
  26.1 0.9 %copy-start.1 = (bf16[128,1024]{1,0:T(8,128)(2,1)S(1)}, bf16[128,1024]{1,0:T(8,128)(2,1)}, u32[]{:S(2)}) copy-start(bf16[128,1024]{1,0:T(8,128)(2,1)} %g_own.1) | copy-start | bytes 786436
  27.0 0.7 copy-start.2
  37.0 1.3 %collective-permute-start.2 = (f32[4,8,512]{2,1,0:T(8,128)S(1)}, f32[4,8,512]{2,1,0:T(8,128)S(1)}, u32[]{:S(2)}, u32[]{:S(2)}) collective-permute-start(f32[4,8,512]{2,1,0:T(8,128)S(1)} %get-tuple-element.18.stats), channel_id=1, source_target_pairs={{0,8},{8,0},{1,9},{9,1},{2,10},{10,2},{3,11},{11,3},{4,12},{12,4},... | collective-permute-start | bytes 196616 | tf_op jit(solution)/shard_map/ppermute | solution.py:240
  47.2 21.5 %all-to-all-start.1 = ((bf16[16,128,256]{2,1,0:T(8,128)(2,1)}), bf16[16,128,256]{2,1,0:T(8,128)(2,1)S(1)}, u32[]{:S(2)}, u32[]{:S(2)}) async-start(bf16[16,128,256]{2,1,0:T(8,128)(2,1)} %bitcast.2), calls=%async_computation.1 | async-start | bytes 2097152 | tf_op jit(solution)/shard_map/all_to_all | solution.py:251
  53.5 1.9 %collective-permute-start.3 = (f32[128,1024]{1,0:T(8,128)S(1)}, f32[128,1024]{1,0:T(8,128)S(1)}, u32[]{:S(2)}, u32[]{:S(2)}) collective-permute-start(f32[128,1024]{1,0:T(8,128)S(1)} %get-tuple-element.25), channel_id=1, source_target_pairs={{0,8},{8,0},{1,9},{9,1},{2,10},{10,2},{3,11},{11,3},{4,12},{12,4},... | collective-permute-start | bytes 1572872 | tf_op jit(solution)/shard_map/ppermute | solution.py:240

commit v3 on v1

v3 whole, which is shorter than its diff:
```python
import jax
import jax.numpy as jnp
from jax import lax
from jax.experimental import pallas as pl
from jax.experimental.pallas import tpu as pltpu
from jax.sharding import Mesh, PartitionSpec as P

HD = 128
QGROUP = 8
BLOCK = 64
TOK = 128
UNITS = 4
ROWS = QGROUP * BLOCK
ALL_ROWS = UNITS * ROWS
LINE = 4 * TOK
LANES = 1024
NEG = -1e30
SCALE = HD**-0.5
LOG2E = 1.4426950408889634
QUERY = 32
BF16 = jnp.bfloat16
F32 = jnp.float32


def mm(a, b):
    return jnp.dot(a, b, preferred_element_type=F32)


def mm_t(a, b):
    return lax.dot_general(a, b, (((1,), (1,)), ((), ())), preferred_element_type=F32)


def fold(x, op):
    return op(op(x.reshape(x.shape[0] // 8, 8, x.shape[1]), axis=0), axis=0, keepdims=True)


def call(kernel, name, ins, outs, scratch, flops, exps, args, limit=10):
    space = {"s": pltpu.SMEM, "v": pltpu.VMEM}
    spec = {k: pl.BlockSpec(memory_space=m) for k, m in space.items()}
    return pl.pallas_call(
        kernel,
        out_shape=tuple(jax.ShapeDtypeStruct(shape, dtype) for _, shape, dtype in outs),
        in_specs=[spec[k] for k in ins],
        out_specs=tuple(spec[k] for k, _, _ in outs),
        scratch_shapes=[space[k](shape, dtype) for k, shape, dtype in scratch],
        compiler_params=pltpu.CompilerParams(vmem_limit_bytes=limit * 2**20),
        cost_estimate=pl.CostEstimate(flops=flops, bytes_accessed=2**20, transcendentals=exps),
        name=name,
    )(*args)


def join(parts):
    def kernel(*refs):
        for i, part in enumerate(refs[:-1]):
            refs[-1][i * TOK : (i + 1) * TOK, :] = part[...]

    return call(kernel, "join", "v" * 4, [("v", (LINE, 2 * HD), BF16)], [], 0, 0, parts)[0]


def prep_kernel(order, place, q_own, q_other, g_own, g_other, meta, rows_qg):
    ctx = place[0]
    core, x, y = lax.rem(ctx, 2), lax.rem(ctx // 2, 4), ctx // 8
    for dy in range(4):
        for dx in range(4):
            chip = lax.rem(y + 4 - dy, 4) * 4 + lax.rem(x + 4 - dx, 4)
            for h in range(2):
                meta[dy * 8 + dx * 2 + h] = order[(chip * 2 + core) * 2 + h]
    for u in range(UNITS):
        meta[QUERY + u] = order[(ctx + (u // 2) * (1 - 2 * core)) * 2 + u % 2]
        q, g = ((q_own, g_own), (q_other, g_other))[u // 2]
        for h in range(QGROUP):
            part = (slice(u % 2 * BLOCK, (u % 2 + 1) * BLOCK), slice(h * HD, (h + 1) * HD))
            rows = slice(u * ROWS + h * BLOCK, u * ROWS + (h + 1) * BLOCK)
            rows_qg[0, rows, :] = q[part]
            rows_qg[1, rows, :] = g[part]


def prepare(order, place, q_own, q_other, g_own, g_other):
    outs = [("s", (QUERY + UNITS,), jnp.int32), ("v", (2, ALL_ROWS, HD), BF16)]
    return call(
        prep_kernel, "prep", "ssvvvv", outs, [], 0, 0, (order, place, q_own, q_other, g_own, g_other)
    )


def merge(a, b):
    top = jnp.maximum(a[0], b[0])
    wa, wb = jnp.exp2(a[0] - top), jnp.exp2(b[0] - top)
    return top, a[1] * wa + b[1] * wb, a[2] * wa + b[2] * wb


def stats_of(ref, lanes=slice(None)):
    return tuple(ref[k : k + 1, lanes] for k in range(3))


def stats_piece(dy, meta, rows_qg, lines, before):
    chunks = len(lines)

    def kernel(meta, rows_qg, *refs):
        lines = refs[:chunks]
        before = refs[chunks] if len(refs) > chunks + 3 else None
        stats, p_all, dp_all = refs[-3:]
        stats[...] = jnp.zeros((8, ALL_ROWS), F32)
        size = LINE // chunks
        for half in range(ALL_ROWS // LANES):
            lanes = slice(half * LANES, (half + 1) * LANES)
            lane = lax.broadcasted_iota(jnp.int32, (1, LANES), 1)
            first, second = meta[QUERY + half * 2], meta[QUERY + half * 2 + 1]
            row_pos = jnp.where(lane < ROWS, first, second) * BLOCK + lax.rem(lane, BLOCK)
            key = lax.broadcasted_iota(jnp.int32, (BLOCK, LANES), 0)
            tops = []
            for c, line in enumerate(lines):
                s = mm_t(line[:, :HD], rows_qg[0, lanes, :]) * (SCALE * LOG2E)
                for b in range(size // BLOCK):
                    base = meta[dy * 8 + c * (size // BLOCK) + b] * BLOCK
                    part = jnp.where(key <= row_pos - base, s[b * BLOCK : (b + 1) * BLOCK], NEG)
                    p_all[c * size + b * BLOCK : c * size + (b + 1) * BLOCK, lanes] = part
                    tops.append(jnp.max(part.reshape(8, 8, LANES), axis=0))
            while len(tops) > 1:
                tops = [jnp.maximum(tops[i], tops[i + 1]) for i in range(0, len(tops), 2)]
            top = jnp.max(tops[0], axis=0, keepdims=True)
            total, delta = jnp.zeros((1, LANES), F32), jnp.zeros((1, LANES), F32)
            for c, line in enumerate(lines):
                rows = slice(c * size, (c + 1) * size)
                dp = mm_t(line[:, HD:], rows_qg[1, lanes, :])
                p = jnp.exp2(p_all[rows, lanes] - top)
                p_all[rows, lanes] = p
                dp_all[rows, lanes] = dp
                total += fold(p, jnp.sum)
                delta += fold(p * dp, jnp.sum)
            stats[3:4, lanes] = top
            now = (top, total, delta)
            if before is not None:
                now = merge(stats_of(before, lanes), now)
            for k in range(3):
                stats[k : k + 1, lanes] = now[k]

    table = ("v", (LINE, ALL_ROWS), F32)
    args = (meta, rows_qg, *lines) + (() if before is None else (before,))
    pairs = LINE * ALL_ROWS
    return call(
        kernel, "stats", "s" + "v" * (len(args) - 1), [("v", (8, ALL_ROWS), F32), table, table], [],
        4 * pairs * HD, pairs, args,
    )


def swapped(came):
    halves = [stats_of(came, slice(h * LANES, (h + 1) * LANES)) for h in (1, 0)]
    return tuple(jnp.concatenate(pair, axis=1) for pair in zip(*halves))


def weights(own, final, came):
    top, total, delta = merge(stats_of(final), swapped(came))
    inv = 1.0 / total
    return jnp.exp2(own[3:4, :] - top) * inv, delta * inv


def grads_piece(rows_qg, piece, final, came, pieces, dtype):
    size = LINE // pieces

    def kernel(rows_qg, own, p_all, dp_all, final, came, *outs):
        w, delta = weights(own, final, came)
        step = 256
        for i in range(LINE // step):
            rows = slice(i * step, (i + 1) * step)
            p = p_all[rows, :] * w
            ds = (p * (dp_all[rows, :] - delta) * SCALE).astype(BF16)
            at = i * step // size
            dst = slice(i * step - at * size, (i + 1) * step - at * size)
            outs[at][dst, HD:] = mm(p.astype(BF16), rows_qg[1]).astype(dtype)
            outs[at][dst, :HD] = mm(ds, rows_qg[0]).astype(dtype)

    outs = [("v", (size, 2 * HD), dtype)] * pieces
    return call(
        kernel, "grads", "v" * 6, outs, [], 4 * LINE * ALL_ROWS * HD, 0, (rows_qg, *piece, final, came)
    )


def add_far(a, b, to_a, to_b):
    half = LINE // 2

    def kernel(a, b, to_a, to_b, out_a, out_b):
        out_a[:half] = a[:half].astype(BF16)
        out_a[half:] = (a[half:] + to_a[...].astype(F32)).astype(BF16)
        out_b[:half] = (b[:half] + to_b[...].astype(F32)).astype(BF16)
        out_b[half:] = b[half:].astype(BF16)

    line = ("v", (LINE, 2 * HD), BF16)
    return call(kernel, "add_far", "v" * 4, [line, line], [], 0, 0, (a, b, to_a, to_b))


def add_near(own, a, b):
    def kernel(own, a, b, *outs):
        for i, out in enumerate(outs):
            rows = slice(i * TOK, (i + 1) * TOK)
            out[...] = (own[rows, :] + a[rows, :].astype(F32) + b[rows, :].astype(F32)).astype(BF16)

    return call(kernel, "add_near", "v" * 3, [("v", (TOK, 2 * HD), BF16)] * 4, [], 0, 0, (own, a, b))


def query_grads(lines, pieces, final, came):
    counts = [len(group) for group in lines]

    def kernel(final, came, *refs):
        dq_own, dq_other, kt, dqt = refs[-4:]
        refs = list(refs[:-4])
        groups = [[refs.pop(0) for _ in range(n)] for n in counts]
        tables = [[refs.pop(0) for _ in range(3)] for _ in counts]
        for j, group in enumerate(groups):
            size = LINE // len(group)
            for c, line in enumerate(group):
                kt[j, :, c * size : (c + 1) * size] = line[:, :HD].T
        for half in range(ALL_ROWS // LANES):
            lanes = slice(half * LANES, (half + 1) * LANES)
            theirs = slice((1 - half) * LANES, (2 - half) * LANES)
            top, total, delta = merge(stats_of(final, lanes), stats_of(came, theirs))
            inv = 1.0 / total
            delta = delta * inv
            for j, (own, p_all, dp_all) in enumerate(tables):
                w = jnp.exp2(own[3:4, lanes] - top) * inv
                ds = (p_all[:, lanes] * w * (dp_all[:, lanes] - delta) * SCALE).astype(BF16)
                part = mm(kt[j], ds)
                dqt[...] = part if j == 0 else dqt[...] + part
            out = dqt[...].T
            for u in range(2):
                for h in range(QGROUP):
                    part = (slice(u * BLOCK, (u + 1) * BLOCK), slice(h * HD, (h + 1) * HD))
                    rows = slice(u * ROWS + h * BLOCK, u * ROWS + (h + 1) * BLOCK)
                    (dq_own, dq_other)[half][part] = out[rows, :]

    args = (final, came) + tuple(x for group in lines for x in group) + tuple(x for piece in pieces for x in piece)
    out = ("v", (TOK, QGROUP * HD), F32)
    scratch = [("v", (4, HD, LINE), BF16), ("v", (HD, LANES), F32)]
    return call(
        kernel, "queries", "v" * len(args), [out, out], scratch, 8 * LINE * ALL_ROWS * HD, 0, args
    )


def shards(queries, keys, values, out_grad, block_order):
    def swap(x):
        return lax.ppermute(x, "core", [(0, 1), (1, 0)])

    def shift(x, axis, s):
        return lax.ppermute(x, axis, [(i, (i + s) % 4) for i in range(4)])

    kv = jnp.concatenate([keys, values], axis=1)
    line = join((kv, shift(kv, "x", 1), shift(kv, "x", 2), shift(kv, "x", 3)))
    up, down = shift(line, "y", 1), shift(line, "y", 3)
    far = (shift(down[: LINE // 2], "y", 3), shift(up[LINE // 2 :], "y", 1))
    place = lax.axis_index(("y", "x", "core")).astype(jnp.int32).reshape(1)
    meta, rows_qg = prepare(block_order, place, queries, swap(queries), out_grad, swap(out_grad))
    lines = ((line,), (up,), (down,), far)
    pieces, before = [], None
    for dy, group in zip((0, 1, 3, 2), lines):
        pieces.append(stats_piece(dy, meta, rows_qg, group, before))
        before = pieces[-1][0]
    came = swap(before)
    far1, far2 = grads_piece(rows_qg, pieces[3], before, came, 2, BF16)
    (up_part,) = grads_piece(rows_qg, pieces[1], before, came, 1, F32)
    (down_part,) = grads_piece(rows_qg, pieces[2], before, came, 1, F32)
    up_sum, down_sum = add_far(up_part, down_part, shift(far2, "y", 3), shift(far1, "y", 1))
    (own_part,) = grads_piece(rows_qg, pieces[0], before, came, 1, F32)
    parts = add_near(own_part, shift(up_sum, "y", 3), shift(down_sum, "y", 1))
    dq_own, dq_other = query_grads(lines, pieces, before, came)
    dq = (dq_own + swap(dq_other)).astype(BF16)
    dkv = parts[0].astype(F32)
    for s in (1, 2, 3):
        dkv = dkv + shift(parts[s], "x", 4 - s).astype(F32)
    mine = jnp.concatenate([dq, dkv.astype(BF16)], axis=1).reshape(8, TOK // 8, 10 * HD)
    got = lax.all_to_all(mine, "head", 0, 0, tiled=True).transpose(1, 0, 2)
    cols = [got[:, :, : 8 * HD], got[:, :, 8 * HD : 9 * HD], got[:, :, 9 * HD :]]
    return jnp.concatenate([c.reshape(TOK // 8, -1) for c in cols], axis=1)


def solution(mesh):
    split = Mesh(mesh.devices.reshape(4, 4, 2, 8), ("y", "x", "core", "head"))
    ctx = ("y", "x", "core")
    rows = P(ctx, "head")
    return jax.shard_map(
        shards,
        mesh=split,
        in_specs=(rows, rows, rows, rows, P()),
        out_specs=P(ctx + ("head",), None),
        check_vma=False,
    )
```

time: 97.4 us -> 77.5 us (0.80)
  blocking collectives: 73 us -> 19.5 us
  starting transfers between devices: 0.1 us -> 21.3 us
  waiting for transfers between devices: 5.3 us -> 11.7 us
  local copies, waits for them, and re-layouts: 0.17 us -> 4.16 us
  Pallas kernels: 16.8 us -> 19.5 us
  other arithmetic: 1.98 us -> 0.87 us
    all_to_all x2 -> x0, blocking collectives: 52.4 us -> none  [the longest x1 29.2 us: shards(): lax.all_to_all(pair.reshape(CHIPS, TOK, 2 * HD), plane, 0, 0, tiled=True)]
    ppermute x2 -> x18, starting transfers between devices: 0.1 us -> 21.3 us  [the longest x14 20.6 us: shift(): return lax.ppermute(x, axis, [(i, (i + s) % 4) for i in range(4)])]
    ppermute x2 -> x18, waiting for transfers between devices: 5.3 us -> 11.7 us  [the longest x14 10.4 us: shift(): return lax.ppermute(x, axis, [(i, (i + s) % 4) for i in range(4)])]
    unnamed x8 -> x9, local copies, waits for them, and re-layouts: 0.05 us -> 3.35 us
    pallas_call x1 -> x13, Pallas kernels: 16.8 us -> 19.5 us  [call(): pl.pallas_call(kernel, out_shape=tuple((jax.ShapeDtypeStruct(shape, dtype...]
    all_to_all x1, blocking collectives: 20.6 us -> 19.5 us  [shards(): got = lax.all_to_all(mine, 'head', 0, 0, tiled=True).transpose(1, 0, 2)]
  transfers between devices with their start and end apart: 2 -> 18, of which waited for: 2 -> 8; matrix products, arithmetic and copies ran while one was open for 0% -> 0% of each run, Pallas kernels for 0% -> 20%
where the time goes in v3:
time: 77.5 us; the launch traced here: 77.2 us
  starting transfers between devices  21.3 us (27%)
  Pallas kernels  19.5 us (25%)
  blocking collectives  19.5 us (25%)
  waiting for transfers between devices  11.7 us (15%)
  local copies, waits for them, and re-layouts  4.16 us (5%)
  other arithmetic  0.87 us (1%)
    ppermute x14, starting transfers between devices, shift(): return lax.ppermute(x, axis, [(i, (i + s) % 4) for i in range(4)])  20.6 us
    all_to_all x1, blocking collectives, shards(): got = lax.all_to_all(mine, 'head', 0, 0, tiled=True).transpose(1, 0, 2)  19.5 us
    pallas_call x13, Pallas kernels, call(): pl.pallas_call(kernel, out_shape=tuple((jax.ShapeDtypeStruct(shape, dtype...  19.5 us
    ppermute x14, waiting for transfers between devices, shift(): return lax.ppermute(x, axis, [(i, (i + s) % 4) for i in range(4)])  10.4 us
    unnamed x9, local copies, waits for them, and re-layouts  3.35 us
  transfers between devices with their start and end apart: 18, of which 8 were waited for; matrix products, arithmetic and copies ran while one was open for 0% of the time, Pallas kernels for 20%

profile of v3, /device:TPU:2, one launch (start us, length us, event | category | flops | bytes accessed | tf_op | source)
XLA Modules:
  0.0 77.2 jit_solution(11735299853501773326)
XLA Ops:
  0.0 0.8 constant_dynamic-update-slice_fusion.1
  0.8 0.8 constant_dynamic-update-slice_fusion.refs_0_
  1.5 2.3 %collective-permute-start.4 = (bf16[128,256]{1,0:T(8,128)(2,1)S(1)}, bf16[128,256]{1,0:T(8,128)(2,1)S(1)}, u32[]{:S(2)}, u32[]{:S(2)}) collective-permute-start(bf16[128,256]{1,0:T(8,128)(2,1)S(1)} %constant_dynamic-update-slice_fusion.refs_0_), channel_id=1, source_target_pairs={{0,48},{16,0},{32,16},{48,32},{1,49},{17,1},{33,17},{49,33},{2,50}... | collective-permute-start | bytes 196616 | tf_op jit(solution)/shard_map/ppermute | solution.py:243
  3.9 0.7 collective-permute-start.3
  4.6 1.8 %collective-permute-start.2 = (bf16[128,256]{1,0:T(8,128)(2,1)S(1)}, bf16[128,256]{1,0:T(8,128)(2,1)S(1)}, u32[]{:S(2)}, u32[]{:S(2)}) collective-permute-start(bf16[128,256]{1,0:T(8,128)(2,1)S(1)} %constant_dynamic-update-slice_fusion.refs_0_), channel_id=1, source_target_pairs={{0,16},{16,32},{32,48},{48,0},{1,17},{17,33},{33,49},{49,1},{2,18}... | collective-permute-start | bytes 196616 | tf_op jit(solution)/shard_map/ppermute | solution.py:243
  6.4 0.0 collective-permute-start
  6.4 0.5 collective-permute-start.1
  6.9 0.0 collective-permute-done.4.refs_3_
  6.9 2.8 %collective-permute-done.3.refs_2_ = bf16[128,256]{1,0:T(8,128)(2,1)S(1)} collective-permute-done((bf16[128,256]{1,0:T(8,128)(2,1)S(1)}, bf16[128,256]{1,0:T(8,128)(2,1)S(1)}, u32[]{:S(2)}, u32[]{:S(2)}) %collective-permute-start.3) | collective-permute-done | bytes 65568 | tf_op jit(solution)/shard_map/ppermute | solution.py:243
  9.6 0.0 collective-permute-done.2.refs_1_
  9.7 0.8 %collective-permute-start.7 = (bf16[512,256]{1,0:T(8,128)(2,1)S(1)}, bf16[512,256]{1,0:T(8,128)(2,1)S(1)}, u32[]{:S(2)}, u32[]{:S(2)}) collective-permute-start(bf16[512,256]{1,0:T(8,128)(2,1)S(1)} %join.1.refs_0_), channel_id=1, source_target_pairs={{0,64},{64,128},{128,192},{192,0},{1,65},{65,129},{129,193},{193,1... | collective-permute-start | bytes 786440 | tf_op jit(solution)/shard_map/ppermute | solution.py:243
  10.5 2.5 %collective-permute-start.5 = (bf16[512,256]{1,0:T(8,128)(2,1)S(1)}, bf16[512,256]{1,0:T(8,128)(2,1)S(1)}, u32[]{:S(2)}, u32[]{:S(2)}) collective-permute-start(bf16[512,256]{1,0:T(8,128)(2,1)S(1)} %join.1.refs_0_), channel_id=1, source_target_pairs={{0,192},{64,0},{128,64},{192,128},{1,193},{65,1},{129,65},{193,129... | collective-permute-start | bytes 786440 | tf_op jit(solution)/shard_map/ppermute | solution.py:243
  13.0 0.0 collective-permute-done.q_other
  13.0 0.0 collective-permute-done.1.g_other
  13.0 0.0 copy-start
  13.0 0.9 %copy-done = bf16[128,1024]{1,0:T(8,128)(2,1)S(1)} copy-done((bf16[128,1024]{1,0:T(8,128)(2,1)S(1)}, bf16[128,1024]{1,0:T(8,128)(2,1)}, u32[]{:S(2)}) %copy-start) | copy-done | bytes 262168
  13.9 0.0 copy-start.1
  13.9 0.9 %copy-done.1 = bf16[128,1024]{1,0:T(8,128)(2,1)S(1)} copy-done((bf16[128,1024]{1,0:T(8,128)(2,1)S(1)}, bf16[128,1024]{1,0:T(8,128)(2,1)}, u32[]{:S(2)}) %copy-start.1) | copy-done | bytes 262168
  14.9 0.0 copy-start.2
  14.9 0.7 copy-done.2
  15.6 1.4 %prep.1 = (s32[36]{0:T(128)S(1)}, bf16[2,2048,128]{2,1,0:T(8,128)(2,1)S(1)}) custom-call(s32[64]{0:T(128)S(1)} %copy-done.2, s32[1]{0:T(128)} %bitcast.place, bf16[128,1024]{1,0:T(8,128)(2,1)S(1)} %copy-done, bf16[128,1024]{1,0:T(8,128)(2,1)S(1)} %collective-permute-done.q_other, bf16[128,1024]{1,0:T(8,128)(2,1)S(1)} %copy-done.1, ...), custom_call_target="tpu_custom_call" | custom-call | bytes 1048576 | tf_op jit(solution)/shard_map/prep/pallas_call | solution.py:40
  16.9 0.4 collective-permute-done.7.refs_0_.refs_1_
  17.3 0.1 collective-permute-start.8
  17.4 0.0 collective-permute-done.5.refs_0_.refs_2_
  17.5 3.5 %collective-permute-start.6 = (bf16[256,256]{1,0:T(8,128)(2,1)S(1)}, bf16[256,256]{1,0:T(8,128)(2,1)S(1)}, u32[]{:S(2)}, u32[]{:S(2)}) collective-permute-start(bf16[256,256]{1,0:T(8,128)(2,1)S(1)} %slice.20), channel_id=1, source_target_pairs={{0,192},{64,0},{128,64},{192,128},{1,193},{65,1},{129,65},{193,129... | collective-permute-start | bytes 393224 | tf_op jit(solution)/shard_map/ppermute | solution.py:243
  20.9 2.2 %stats.4 = (f32[8,2048]{1,0:T(8,128)S(1)}, f32[512,2048]{1,0:T(8,128)S(1)}, f32[512,2048]{1,0:T(8,128)S(1)}) custom-call(s32[36]{0:T(128)S(1)} %get-tuple-element.29.meta, bf16[2,2048,128]{2,1,0:T(8,128)(2,1)S(1)} %get-tuple-element.30.rows_qg, bf16[512,256]{1,0:T(8,128)(2,1)S(1)} %join.1.refs_0_), custom_call_target="tpu_custom_call" | custom-call | flops 536870912 | bytes 1048576 | tf_op jit(solution)/shard_map/stats/pallas_call | solution.py:40
  23.2 2.3 %stats.5 = (f32[8,2048]{1,0:T(8,128)S(1)}, f32[512,2048]{1,0:T(8,128)S(1)}, f32[512,2048]{1,0:T(8,128)S(1)}) custom-call(s32[36]{0:T(128)S(1)} %get-tuple-element.29.meta, bf16[2,2048,128]{2,1,0:T(8,128)(2,1)S(1)} %get-tuple-element.30.rows_qg, bf16[512,256]{1,0:T(8,128)(2,1)S(1)} %collective-permute-done.7.refs_0_.refs_1_, ...), custom_call_target="tpu_custom_call" | custom-call | flops 536870912 | bytes 1048576 | tf_op jit(solution)/shard_map/stats/pallas_call | solution.py:40
  25.5 2.3 %stats.6 = (f32[8,2048]{1,0:T(8,128)S(1)}, f32[512,2048]{1,0:T(8,128)S(1)}, f32[512,2048]{1,0:T(8,128)S(1)}) custom-call(s32[36]{0:T(128)S(1)} %get-tuple-element.29.meta, bf16[2,2048,128]{2,1,0:T(8,128)(2,1)S(1)} %get-tuple-element.30.rows_qg, bf16[512,256]{1,0:T(8,128)(2,1)S(1)} %collective-permute-done.5.refs_0_.refs_2_, ...), custom_call_target="tpu_custom_call" | custom-call | flops 536870912 | bytes 1048576 | tf_op jit(solution)/shard_map/stats/pallas_call | solution.py:40
  27.7 0.0 collective-permute-done.8.refs_1_.refs_4_
  27.8 0.0 collective-permute-done.6.refs_0_.refs_3_
  27.8 2.3 %stats.7 = (f32[8,2048]{1,0:T(8,128)S(1)}, f32[512,2048]{1,0:T(8,128)S(1)}, f32[512,2048]{1,0:T(8,128)S(1)}) custom-call(s32[36]{0:T(128)S(1)} %get-tuple-element.29.meta, bf16[2,2048,128]{2,1,0:T(8,128)(2,1)S(1)} %get-tuple-element.30.rows_qg, bf16[256,256]{1,0:T(8,128)(2,1)S(1)} %collective-permute-done.6.refs_0_.refs_3_, ...), custom_call_target="tpu_custom_call" | custom-call | flops 536870912 | bytes 1048576 | tf_op jit(solution)/shard_map/stats/pallas_call | solution.py:40
  30.1 0.1 collective-permute-start.9
  30.2 1.2 %collective-permute-done.9.came = f32[8,2048]{1,0:T(8,128)S(1)} collective-permute-done((f32[8,2048]{1,0:T(8,128)S(1)}, f32[8,2048]{1,0:T(8,128)S(1)}, u32[]{:S(2)}, u32[]{:S(2)}) %collective-permute-start.9) | collective-permute-done | bytes 65568 | tf_op jit(solution)/shard_map/ppermute | solution.py:240
  31.4 1.4 %grads.7 = (bf16[256,256]{1,0:T(8,128)(2,1)S(1)}, bf16[256,256]{1,0:T(8,128)(2,1)S(1)}) custom-call(bf16[2,2048,128]{2,1,0:T(8,128)(2,1)S(1)} %get-tuple-element.30.rows_qg, f32[8,2048]{1,0:T(8,128)S(1)} %get-tuple-element.34.final.refs_14_.own, f32[512,2048]{1,0:T(8,128)S(1)} %get-tuple-element.41.refs_15_.p_all, ...), custom_call_target="tpu_custom_call" | custom-call | flops 536870912 | bytes 1048576 | tf_op jit(solution)/shard_map/grads/pallas_call | solution.py:40
  32.8 0.2 collective-permute-start.11
  33.0 1.9 %collective-permute-start.12 = (bf16[256,256]{1,0:T(8,128)(2,1)S(1)}, bf16[256,256]{1,0:T(8,128)(2,1)S(1)}, u32[]{:S(2)}, u32[]{:S(2)}) collective-permute-start(bf16[256,256]{1,0:T(8,128)(2,1)S(1)} %get-tuple-element.46), channel_id=1, source_target_pairs={{0,64},{64,128},{128,192},{192,0},{1,65},{65,129},{129,193},{193,1... | collective-permute-start | bytes 393224 | tf_op jit(solution)/shard_map/ppermute | solution.py:243
  34.9 1.4 %grads.6.b = f32[512,256]{1,0:T(8,128)S(1)} custom-call(bf16[2,2048,128]{2,1,0:T(8,128)(2,1)S(1)} %get-tuple-element.30.rows_qg, f32[8,2048]{1,0:T(8,128)S(1)} %get-tuple-element.33.refs_2_.refs_11_.own, f32[512,2048]{1,0:T(8,128)S(1)} %get-tuple-element.39.refs_12_.p_all, f32[512,2048]{1,0:T(8,128)S(1)} %get-tuple-element.40.refs_13_.dp_all, ...), custom_call_target="tpu_custom_call" | custom-call | flops 536870912 | bytes 1048576 | tf_op jit(solution)/shard_map/grads/pallas_call | solution.py:40
  36.2 1.4 %grads.5.a = f32[512,256]{1,0:T(8,128)S(1)} custom-call(bf16[2,2048,128]{2,1,0:T(8,128)(2,1)S(1)} %get-tuple-element.30.rows_qg, f32[8,2048]{1,0:T(8,128)S(1)} %get-tuple-element.32.refs_1_.refs_8_.own, f32[512,2048]{1,0:T(8,128)S(1)} %get-tuple-element.37.refs_9_.p_all, f32[512,2048]{1,0:T(8,128)S(1)} %get-tuple-element.38.refs_10_.dp_all, ...), custom_call_target="tpu_custom_call" | custom-call | flops 536870912 | bytes 1048576 | tf_op jit(solution)/shard_map/grads/pallas_call | solution.py:40
  37.6 0.8 %collective-permute-done.11.to_a = bf16[256,256]{1,0:T(8,128)(2,1)S(1)} collective-permute-done((bf16[256,256]{1,0:T(8,128)(2,1)S(1)}, bf16[256,256]{1,0:T(8,128)(2,1)S(1)}, u32[]{:S(2)}, u32[]{:S(2)}) %collective-permute-start.11) | collective-permute-done | bytes 131104 | tf_op jit(solution)/shard_map/ppermute | solution.py:243
  38.4 1.5 %collective-permute-done.12.to_b = bf16[256,256]{1,0:T(8,128)(2,1)S(1)} collective-permute-done((bf16[256,256]{1,0:T(8,128)(2,1)S(1)}, bf16[256,256]{1,0:T(8,128)(2,1)S(1)}, u32[]{:S(2)}, u32[]{:S(2)}) %collective-permute-start.12) | collective-permute-done | bytes 131104 | tf_op jit(solution)/shard_map/ppermute | solution.py:243
  39.9 0.1 add_far.1
  40.0 0.1 collective-permute-start.13
  40.1 2.0 %collective-permute-start.14 = (bf16[512,256]{1,0:T(8,128)(2,1)S(1)}, bf16[512,256]{1,0:T(8,128)(2,1)S(1)}, u32[]{:S(2)}, u32[]{:S(2)}) collective-permute-start(bf16[512,256]{1,0:T(8,128)(2,1)S(1)} %get-tuple-element.48), channel_id=1, source_target_pairs={{0,64},{64,128},{128,192},{192,0},{1,65},{65,129},{129,193},{193,1... | collective-permute-start | bytes 786440 | tf_op jit(solution)/shard_map/ppermute | solution.py:243
  42.1 3.4 %queries.1 = (f32[128,1024]{1,0:T(8,128)S(1)}, f32[128,1024]{1,0:T(8,128)S(1)}) custom-call(f32[8,2048]{1,0:T(8,128)S(1)} %get-tuple-element.34.final.refs_14_.own, f32[8,2048]{1,0:T(8,128)S(1)} %collective-permute-done.9.came, bf16[512,256]{1,0:T(8,128)(2,1)S(1)} %join.1.refs_0_, bf16[512,256]{1,0:T(8,128)(2,1)S(1)} %collective-permute-done.7.refs_0_.refs_1_, ...), custom_call_target="tpu_custom_call" | custom-call | flops 1073741824 | bytes 1048576 | tf_op jit(solution)/shard_map/queries/pallas_call | solution.py:40
  45.5 0.1 collective-permute-start.10
  45.6 1.4 %grads.4.own = f32[512,256]{1,0:T(8,128)S(1)} custom-call(bf16[2,2048,128]{2,1,0:T(8,128)(2,1)S(1)} %get-tuple-element.30.rows_qg, f32[8,2048]{1,0:T(8,128)S(1)} %get-tuple-element.31.refs_1_.refs_5_.own, f32[512,2048]{1,0:T(8,128)S(1)} %get-tuple-element.35.refs_6_.p_all, f32[512,2048]{1,0:T(8,128)S(1)} %get-tuple-element.36.refs_7_.dp_all, ...), custom_call_target="tpu_custom_call" | custom-call | flops 536870912 | bytes 1048576 | tf_op jit(solution)/shard_map/grads/pallas_call | solution.py:40
  47.0 0.6 collective-permute-done.13.a
  47.6 1.3 %collective-permute-done.14.b = bf16[512,256]{1,0:T(8,128)(2,1)S(1)} collective-permute-done((bf16[512,256]{1,0:T(8,128)(2,1)S(1)}, bf16[512,256]{1,0:T(8,128)(2,1)S(1)}, u32[]{:S(2)}, u32[]{:S(2)}) %collective-permute-start.14) | collective-permute-done | bytes 262176 | tf_op jit(solution)/shard_map/ppermute | solution.py:243
  48.9 0.1 add_near.1
  49.0 2.0 %collective-permute-start.15 = (bf16[128,256]{1,0:T(8,128)(2,1)S(1)}, bf16[128,256]{1,0:T(8,128)(2,1)S(1)}, u32[]{:S(2)}, u32[]{:S(2)}) collective-permute-start(bf16[128,256]{1,0:T(8,128)(2,1)S(1)} %get-tuple-element.50), channel_id=1, source_target_pairs={{0,48},{16,0},{32,16},{48,32},{1,49},{17,1},{33,17},{49,33},{2,50}... | collective-permute-start | bytes 196616 | tf_op jit(solution)/shard_map/ppermute | solution.py:243
  50.9 1.2 %collective-permute-start.16 = (bf16[128,256]{1,0:T(8,128)(2,1)S(1)}, bf16[128,256]{1,0:T(8,128)(2,1)S(1)}, u32[]{:S(2)}, u32[]{:S(2)}) collective-permute-start(bf16[128,256]{1,0:T(8,128)(2,1)S(1)} %get-tuple-element.51), channel_id=1, source_target_pairs={{0,32},{16,48},{32,0},{48,16},{1,33},{17,49},{33,1},{49,17},{2,34}... | collective-permute-start | bytes 196616 | tf_op jit(solution)/shard_map/ppermute | solution.py:243
  52.1 1.6 %collective-permute-start.17 = (bf16[128,256]{1,0:T(8,128)(2,1)S(1)}, bf16[128,256]{1,0:T(8,128)(2,1)S(1)}, u32[]{:S(2)}, u32[]{:S(2)}) collective-permute-start(bf16[128,256]{1,0:T(8,128)(2,1)S(1)} %get-tuple-element.52), channel_id=1, source_target_pairs={{0,16},{16,32},{32,48},{48,0},{1,17},{17,33},{33,49},{49,1},{2,18}... | collective-permute-start | bytes 196616 | tf_op jit(solution)/shard_map/ppermute | solution.py:243
  53.7 0.0 collective-permute-done.15
  53.7 3.0 %collective-permute-done.16 = bf16[128,256]{1,0:T(8,128)(2,1)S(1)} collective-permute-done((bf16[128,256]{1,0:T(8,128)(2,1)S(1)}, bf16[128,256]{1,0:T(8,128)(2,1)S(1)}, u32[]{:S(2)}, u32[]{:S(2)}) %collective-permute-start.16) | collective-permute-done | bytes 65568 | tf_op jit(solution)/shard_map/ppermute | solution.py:243
  56.7 0.0 collective-permute-done.17
  56.8 0.0 collective-permute-done.10
  56.8 0.1 add_convert_fusion
  56.9 19.5 %all_to_all.5 = bf16[8,16,1280]{2,1,0:T(8,128)(2,1)S(1)} all-to-all(bf16[8,16,1280]{2,1,0:T(8,128)(2,1)S(1)} %bitcast.16), channel_id=1, replica_groups=mesh['y'=4,'x'=4,'core'=2,'head'=8] {'head'}, dimensions={0} | all-to-all | bytes 655360 | tf_op jit(solution)/shard_map/all_to_all | solution.py:269
  76.5 0.7 pad_maximum_fusion.1
  (9 shorter events, 0.2 us)
Async XLA Ops:
  1.5 5.3 %collective-permute-start.4 = (bf16[128,256]{1,0:T(8,128)(2,1)S(1)}, bf16[128,256]{1,0:T(8,128)(2,1)S(1)}, u32[]{:S(2)}, u32[]{:S(2)}) collective-permute-start(bf16[128,256]{1,0:T(8,128)(2,1)S(1)} %constant_dynamic-update-slice_fusion.refs_0_), channel_id=1, source_target_pairs={{0,48},{16,0},{32,16},{48,32},{1,49},{17,1},{33,17},{49,33},{2,50}... | collective-permute-start | bytes 196616 | tf_op jit(solution)/shard_map/ppermute | solution.py:243
  3.9 5.8 %collective-permute-start.3 = (bf16[128,256]{1,0:T(8,128)(2,1)S(1)}, bf16[128,256]{1,0:T(8,128)(2,1)S(1)}, u32[]{:S(2)}, u32[]{:S(2)}) collective-permute-start(bf16[128,256]{1,0:T(8,128)(2,1)S(1)} %constant_dynamic-update-slice_fusion.refs_0_), channel_id=1, source_target_pairs={{0,32},{16,48},{32,0},{48,16},{1,33},{17,49},{33,1},{49,17},{2,34}... | collective-permute-start | bytes 196616 | tf_op jit(solution)/shard_map/ppermute | solution.py:243
  4.6 5.1 %collective-permute-start.2 = (bf16[128,256]{1,0:T(8,128)(2,1)S(1)}, bf16[128,256]{1,0:T(8,128)(2,1)S(1)}, u32[]{:S(2)}, u32[]{:S(2)}) collective-permute-start(bf16[128,256]{1,0:T(8,128)(2,1)S(1)} %constant_dynamic-update-slice_fusion.refs_0_), channel_id=1, source_target_pairs={{0,16},{16,32},{32,48},{48,0},{1,17},{17,33},{33,49},{49,1},{2,18}... | collective-permute-start | bytes 196616 | tf_op jit(solution)/shard_map/ppermute | solution.py:243
  6.4 6.6 %collective-permute-start = (bf16[128,1024]{1,0:T(8,128)(2,1)}, bf16[128,1024]{1,0:T(8,128)(2,1)S(1)}, u32[]{:S(2)}, u32[]{:S(2)}) collective-permute-start(bf16[128,1024]{1,0:T(8,128)(2,1)} %q_own.1), channel_id=1, source_target_pairs={{0,8},{8,0},{1,9},{9,1},{2,10},{10,2},{3,11},{11,3},{4,12},{12,4},... | collective-permute-start | bytes 786440 | tf_op jit(solution)/shard_map/ppermute | solution.py:240
  6.4 6.6 %collective-permute-start.1 = (bf16[128,1024]{1,0:T(8,128)(2,1)}, bf16[128,1024]{1,0:T(8,128)(2,1)S(1)}, u32[]{:S(2)}, u32[]{:S(2)}) collective-permute-start(bf16[128,1024]{1,0:T(8,128)(2,1)} %g_own.1), channel_id=1, source_target_pairs={{0,8},{8,0},{1,9},{9,1},{2,10},{10,2},{3,11},{11,3},{4,12},{12,4},... | collective-permute-start | bytes 786440 | tf_op jit(solution)/shard_map/ppermute | solution.py:240
  9.7 7.7 %collective-permute-start.7 = (bf16[512,256]{1,0:T(8,128)(2,1)S(1)}, bf16[512,256]{1,0:T(8,128)(2,1)S(1)}, u32[]{:S(2)}, u32[]{:S(2)}) collective-permute-start(bf16[512,256]{1,0:T(8,128)(2,1)S(1)} %join.1.refs_0_), channel_id=1, source_target_pairs={{0,64},{64,128},{128,192},{192,0},{1,65},{65,129},{129,193},{193,1... | collective-permute-start | bytes 786440 | tf_op jit(solution)/shard_map/ppermute | solution.py:243
  10.5 6.9 %collective-permute-start.5 = (bf16[512,256]{1,0:T(8,128)(2,1)S(1)}, bf16[512,256]{1,0:T(8,128)(2,1)S(1)}, u32[]{:S(2)}, u32[]{:S(2)}) collective-permute-start(bf16[512,256]{1,0:T(8,128)(2,1)S(1)} %join.1.refs_0_), channel_id=1, source_target_pairs={{0,192},{64,0},{128,64},{192,128},{1,193},{65,1},{129,65},{193,129... | collective-permute-start | bytes 786440 | tf_op jit(solution)/shard_map/ppermute | solution.py:243
  13.0 1.0 %copy-start = (bf16[128,1024]{1,0:T(8,128)(2,1)S(1)}, bf16[128,1024]{1,0:T(8,128)(2,1)}, u32[]{:S(2)}) copy-start(bf16[128,1024]{1,0:T(8,128)(2,1)} %q_own.1) | copy-start | bytes 786436
  13.9 0.9 %copy-start.1 = (bf16[128,1024]{1,0:T(8,128)(2,1)S(1)}, bf16[128,1024]{1,0:T(8,128)(2,1)}, u32[]{:S(2)}) copy-start(bf16[128,1024]{1,0:T(8,128)(2,1)} %g_own.1) | copy-start | bytes 786436
  14.9 0.7 copy-start.2
  17.3 10.4 %collective-permute-start.8 = (bf16[256,256]{1,0:T(8,128)(2,1)S(1)}, bf16[256,256]{1,0:T(8,128)(2,1)S(1)}, u32[]{:S(2)}, u32[]{:S(2)}) collective-permute-start(bf16[256,256]{1,0:T(8,128)(2,1)S(1)} %slice.21), channel_id=1, source_target_pairs={{0,64},{64,128},{128,192},{192,0},{1,65},{65,129},{129,193},{193,1... | collective-permute-start | bytes 393224 | tf_op jit(solution)/shard_map/ppermute | solution.py:243
  17.5 10.3 %collective-permute-start.6 = (bf16[256,256]{1,0:T(8,128)(2,1)S(1)}, bf16[256,256]{1,0:T(8,128)(2,1)S(1)}, u32[]{:S(2)}, u32[]{:S(2)}) collective-permute-start(bf16[256,256]{1,0:T(8,128)(2,1)S(1)} %slice.20), channel_id=1, source_target_pairs={{0,192},{64,0},{128,64},{192,128},{1,193},{65,1},{129,65},{193,129... | collective-permute-start | bytes 393224 | tf_op jit(solution)/shard_map/ppermute | solution.py:243
  30.1 1.3 %collective-permute-start.9 = (f32[8,2048]{1,0:T(8,128)S(1)}, f32[8,2048]{1,0:T(8,128)S(1)}, u32[]{:S(2)}, u32[]{:S(2)}) collective-permute-start(f32[8,2048]{1,0:T(8,128)S(1)} %get-tuple-element.34.final.refs_14_.own), channel_id=1, source_target_pairs={{0,8},{8,0},{1,9},{9,1},{2,10},{10,2},{3,11},{11,3},{4,12},{12,4},... | collective-permute-start | bytes 196616 | tf_op jit(solution)/shard_map/ppermute | solution.py:240
  32.8 5.6 %collective-permute-start.11 = (bf16[256,256]{1,0:T(8,128)(2,1)S(1)}, bf16[256,256]{1,0:T(8,128)(2,1)S(1)}, u32[]{:S(2)}, u32[]{:S(2)}) collective-permute-start(bf16[256,256]{1,0:T(8,128)(2,1)S(1)} %get-tuple-element.45), channel_id=1, source_target_pairs={{0,192},{64,0},{128,64},{192,128},{1,193},{65,1},{129,65},{193,129... | collective-permute-start | bytes 393224 | tf_op jit(solution)/shard_map/ppermute | solution.py:243
  33.0 7.0 %collective-permute-start.12 = (bf16[256,256]{1,0:T(8,128)(2,1)S(1)}, bf16[256,256]{1,0:T(8,128)(2,1)S(1)}, u32[]{:S(2)}, u32[]{:S(2)}) collective-permute-start(bf16[256,256]{1,0:T(8,128)(2,1)S(1)} %get-tuple-element.46), channel_id=1, source_target_pairs={{0,64},{64,128},{128,192},{192,0},{1,65},{65,129},{129,193},{193,1... | collective-permute-start | bytes 393224 | tf_op jit(solution)/shard_map/ppermute | solution.py:243
  40.0 7.6 %collective-permute-start.13 = (bf16[512,256]{1,0:T(8,128)(2,1)S(1)}, bf16[512,256]{1,0:T(8,128)(2,1)S(1)}, u32[]{:S(2)}, u32[]{:S(2)}) collective-permute-start(bf16[512,256]{1,0:T(8,128)(2,1)S(1)} %get-tuple-element.47), channel_id=1, source_target_pairs={{0,192},{64,0},{128,64},{192,128},{1,193},{65,1},{129,65},{193,129... | collective-permute-start | bytes 786440 | tf_op jit(solution)/shard_map/ppermute | solution.py:243
  40.1 8.8 %collective-permute-start.14 = (bf16[512,256]{1,0:T(8,128)(2,1)S(1)}, bf16[512,256]{1,0:T(8,128)(2,1)S(1)}, u32[]{:S(2)}, u32[]{:S(2)}) collective-permute-start(bf16[512,256]{1,0:T(8,128)(2,1)S(1)} %get-tuple-element.48), channel_id=1, source_target_pairs={{0,64},{64,128},{128,192},{192,0},{1,65},{65,129},{129,193},{193,1... | collective-permute-start | bytes 786440 | tf_op jit(solution)/shard_map/ppermute | solution.py:243
  45.5 11.3 %collective-permute-start.10 = (f32[128,1024]{1,0:T(8,128)S(1)}, f32[128,1024]{1,0:T(8,128)S(1)}, u32[]{:S(2)}, u32[]{:S(2)}) collective-permute-start(f32[128,1024]{1,0:T(8,128)S(1)} %get-tuple-element.44), channel_id=1, source_target_pairs={{0,8},{8,0},{1,9},{9,1},{2,10},{10,2},{3,11},{11,3},{4,12},{12,4},... | collective-permute-start | bytes 1572872 | tf_op jit(solution)/shard_map/ppermute | solution.py:240
  49.0 4.7 %collective-permute-start.15 = (bf16[128,256]{1,0:T(8,128)(2,1)S(1)}, bf16[128,256]{1,0:T(8,128)(2,1)S(1)}, u32[]{:S(2)}, u32[]{:S(2)}) collective-permute-start(bf16[128,256]{1,0:T(8,128)(2,1)S(1)} %get-tuple-element.50), channel_id=1, source_target_pairs={{0,48},{16,0},{32,16},{48,32},{1,49},{17,1},{33,17},{49,33},{2,50}... | collective-permute-start | bytes 196616 | tf_op jit(solution)/shard_map/ppermute | solution.py:243
  50.9 5.8 %collective-permute-start.16 = (bf16[128,256]{1,0:T(8,128)(2,1)S(1)}, bf16[128,256]{1,0:T(8,128)(2,1)S(1)}, u32[]{:S(2)}, u32[]{:S(2)}) collective-permute-start(bf16[128,256]{1,0:T(8,128)(2,1)S(1)} %get-tuple-element.51), channel_id=1, source_target_pairs={{0,32},{16,48},{32,0},{48,16},{1,33},{17,49},{33,1},{49,17},{2,34}... | collective-permute-start | bytes 196616 | tf_op jit(solution)/shard_map/ppermute | solution.py:243
  52.1 4.6 %collective-permute-start.17 = (bf16[128,256]{1,0:T(8,128)(2,1)S(1)}, bf16[128,256]{1,0:T(8,128)(2,1)S(1)}, u32[]{:S(2)}, u32[]{:S(2)}) collective-permute-start(bf16[128,256]{1,0:T(8,128)(2,1)S(1)} %get-tuple-element.52), channel_id=1, source_target_pairs={{0,16},{16,32},{32,48},{48,0},{1,17},{17,33},{33,49},{49,1},{2,18}... | collective-permute-start | bytes 196616 | tf_op jit(solution)/shard_map/ppermute | solution.py:243

commit v4 on v3

--- a/solution.py
+++ b/solution.py
@@ -101,32 +101,46 @@
         stats, p_all, dp_all = refs[-3:]
         stats[...] = jnp.zeros((8, ALL_ROWS), F32)
         size = LINE // chunks
+        def bias(half, kb):
+            base = meta[dy * 8 + kb]
+            cost = [jnp.where(base <= meta[QUERY + half * 2 + u], 0.0, -NEG).astype(F32) for u in range(2)]
+            lane = lax.broadcasted_iota(jnp.int32, (1, LANES), 1)
+            return jnp.where(lane < ROWS, cost[0], cost[1])
+
         for half in range(ALL_ROWS // LANES):
             lanes = slice(half * LANES, (half + 1) * LANES)
-            lane = lax.broadcasted_iota(jnp.int32, (1, LANES), 1)
-            first, second = meta[QUERY + half * 2], meta[QUERY + half * 2 + 1]
-            row_pos = jnp.where(lane < ROWS, first, second) * BLOCK + lax.rem(lane, BLOCK)
-            key = lax.broadcasted_iota(jnp.int32, (BLOCK, LANES), 0)
+            biases = [bias(half, kb) for kb in range(LINE // BLOCK)]
             tops = []
             for c, line in enumerate(lines):
                 s = mm_t(line[:, :HD], rows_qg[0, lanes, :]) * (SCALE * LOG2E)
                 for b in range(size // BLOCK):
-                    base = meta[dy * 8 + c * (size // BLOCK) + b] * BLOCK
-                    part = jnp.where(key <= row_pos - base, s[b * BLOCK : (b + 1) * BLOCK], NEG)
-                    p_all[c * size + b * BLOCK : c * size + (b + 1) * BLOCK, lanes] = part
-                    tops.append(jnp.max(part.reshape(8, 8, LANES), axis=0))
+                    kb = c * (size // BLOCK) + b
+                    part = s[b * BLOCK : (b + 1) * BLOCK]
+                    if dy == 0 and half == 0 and kb < 2:
+                        key = lax.broadcasted_iota(jnp.int32, (BLOCK, ROWS), 0)
+                        row = lax.rem(lax.broadcasted_iota(jnp.int32, (BLOCK, ROWS), 1), BLOCK)
+                        cut = [part[:, :ROWS], part[:, ROWS:]]
+                        cut[kb] = jnp.where(key <= row, cut[kb], NEG)
+                        part = jnp.concatenate(cut, axis=1)
+                    p_all[kb * BLOCK : (kb + 1) * BLOCK, lanes] = part
+                    tops.append(jnp.max(part.reshape(8, 8, LANES), axis=0) - biases[kb])
             while len(tops) > 1:
                 tops = [jnp.maximum(tops[i], tops[i + 1]) for i in range(0, len(tops), 2)]
             top = jnp.max(tops[0], axis=0, keepdims=True)
-            total, delta = jnp.zeros((1, LANES), F32), jnp.zeros((1, LANES), F32)
+            total, delta = jnp.zeros((8, LANES), F32), jnp.zeros((8, LANES), F32)
             for c, line in enumerate(lines):
-                rows = slice(c * size, (c + 1) * size)
                 dp = mm_t(line[:, HD:], rows_qg[1, lanes, :])
-                p = jnp.exp2(p_all[rows, lanes] - top)
-                p_all[rows, lanes] = p
-                dp_all[rows, lanes] = dp
-                total += fold(p, jnp.sum)
-                delta += fold(p * dp, jnp.sum)
+                for b in range(size // BLOCK):
+                    kb = c * (size // BLOCK) + b
+                    rows = slice(kb * BLOCK, (kb + 1) * BLOCK)
+                    dp_part = dp[b * BLOCK : (b + 1) * BLOCK]
+                    p = jnp.exp2(p_all[rows, lanes] - (top + 3.0 * biases[kb]))
+                    p_all[rows, lanes] = p
+                    dp_all[rows, lanes] = dp_part
+                    total += jnp.sum(p.reshape(8, 8, LANES), axis=0)
+                    delta += jnp.sum((p * dp_part).reshape(8, 8, LANES), axis=0)
+            total = jnp.sum(total, axis=0, keepdims=True)
+            delta = jnp.sum(delta, axis=0, keepdims=True)
             stats[3:4, lanes] = top
             now = (top, total, delta)
             if before is not None:
@@ -242,7 +256,8 @@
     def shift(x, axis, s):
         return lax.ppermute(x, axis, [(i, (i + s) % 4) for i in range(4)])
 
-    kv = jnp.concatenate([keys, values], axis=1)
+    low = jnp.asarray(-jnp.inf, BF16)
+    kv = jnp.maximum(lax.pad(keys, low, ((0, 0, 0), (0, HD, 0))), lax.pad(values, low, ((0, 0, 0), (HD, 0, 0))))
     line = join((kv, shift(kv, "x", 1), shift(kv, "x", 2), shift(kv, "x", 3)))
     up, down = shift(line, "y", 1), shift(line, "y", 3)
     far = (shift(down[: LINE // 2], "y", 3), shift(up[LINE // 2 :], "y", 1))

time: 77.5 us -> 76 us (0.981)
  local copies, waits for them, and re-layouts: 4.16 us -> 2.63 us
  Pallas kernels: 19.5 us -> 18.7 us
  other arithmetic: 0.87 us -> 1.65 us
    max x0 -> x1, other arithmetic: none -> 0.78 us  [shards(): jnp.maximum(lax.pad(keys, low, ((0, 0, 0), (0, HD, 0))), lax.pad(values,...]
    unnamed x9 -> x8, local copies, waits for them, and re-layouts: 3.35 us -> 2.58 us
where the time goes in v4:
time: 76 us; the launch traced here: 75.8 us
  starting transfers between devices  21.3 us (28%)
  blocking collectives  19.5 us (26%)
  Pallas kernels  18.7 us (25%)
  waiting for transfers between devices  11.7 us (15%)
  local copies, waits for them, and re-layouts  2.63 us (3%)
  other arithmetic  1.65 us (2%)
    ppermute x14, starting transfers between devices, shift(): return lax.ppermute(x, axis, [(i, (i + s) % 4) for i in range(4)])  20.6 us
    all_to_all x1, blocking collectives, shards(): got = lax.all_to_all(mine, 'head', 0, 0, tiled=True).transpose(1, 0, 2)  19.5 us
    pallas_call x13, Pallas kernels, call(): pl.pallas_call(kernel, out_shape=tuple((jax.ShapeDtypeStruct(shape, dtype...  18.7 us
    ppermute x14, waiting for transfers between devices, shift(): return lax.ppermute(x, axis, [(i, (i + s) % 4) for i in range(4)])  10.4 us
    unnamed x8, local copies, waits for them, and re-layouts  2.58 us
  transfers between devices with their start and end apart: 18, of which 8 were waited for; matrix products, arithmetic and copies ran while one was open for 0% of the time, Pallas kernels for 20%

profile of v4, /device:TPU:2, one launch (start us, length us, event | category | flops | bytes accessed | tf_op | source)
XLA Modules:
  0.0 75.8 jit_solution(10947959601053711337)
XLA Ops:
  0.0 0.8 %pad_maximum_fusion.2.refs_0_ = bf16[128,256]{1,0:T(8,128)(2,1)S(1)} fusion(bf16[128,128]{1,0:T(8,128)(2,1)} %param.7, bf16[128,128]{1,0:T(8,128)(2,1)} %param.6), kind=kLoop, calls=%fused_computation.5 | loop fusion | flops 131072 | bytes 131072 | tf_op jit(solution)/shard_map/max | solution.py:260
  0.8 2.3 %collective-permute-start.4 = (bf16[128,256]{1,0:T(8,128)(2,1)S(1)}, bf16[128,256]{1,0:T(8,128)(2,1)S(1)}, u32[]{:S(2)}, u32[]{:S(2)}) collective-permute-start(bf16[128,256]{1,0:T(8,128)(2,1)S(1)} %pad_maximum_fusion.2.refs_0_), channel_id=1, source_target_pairs={{0,48},{16,0},{32,16},{48,32},{1,49},{17,1},{33,17},{49,33},{2,50}... | collective-permute-start | bytes 196616 | tf_op jit(solution)/shard_map/ppermute | solution.py:257
  3.1 0.7 collective-permute-start.3
  3.8 1.8 %collective-permute-start.2 = (bf16[128,256]{1,0:T(8,128)(2,1)S(1)}, bf16[128,256]{1,0:T(8,128)(2,1)S(1)}, u32[]{:S(2)}, u32[]{:S(2)}) collective-permute-start(bf16[128,256]{1,0:T(8,128)(2,1)S(1)} %pad_maximum_fusion.2.refs_0_), channel_id=1, source_target_pairs={{0,16},{16,32},{32,48},{48,0},{1,17},{17,33},{33,49},{49,1},{2,18}... | collective-permute-start | bytes 196616 | tf_op jit(solution)/shard_map/ppermute | solution.py:257
  5.6 0.0 collective-permute-start
  5.6 0.5 collective-permute-start.1
  6.1 0.0 collective-permute-done.4.refs_3_
  6.1 2.8 %collective-permute-done.3.refs_2_ = bf16[128,256]{1,0:T(8,128)(2,1)S(1)} collective-permute-done((bf16[128,256]{1,0:T(8,128)(2,1)S(1)}, bf16[128,256]{1,0:T(8,128)(2,1)S(1)}, u32[]{:S(2)}, u32[]{:S(2)}) %collective-permute-start.3) | collective-permute-done | bytes 65568 | tf_op jit(solution)/shard_map/ppermute | solution.py:257
  8.9 0.0 collective-permute-done.2.refs_1_
  8.9 0.8 %collective-permute-start.7 = (bf16[512,256]{1,0:T(8,128)(2,1)S(1)}, bf16[512,256]{1,0:T(8,128)(2,1)S(1)}, u32[]{:S(2)}, u32[]{:S(2)}) collective-permute-start(bf16[512,256]{1,0:T(8,128)(2,1)S(1)} %join.1.refs_0_), channel_id=1, source_target_pairs={{0,64},{64,128},{128,192},{192,0},{1,65},{65,129},{129,193},{193,1... | collective-permute-start | bytes 786440 | tf_op jit(solution)/shard_map/ppermute | solution.py:257
  9.8 2.5 %collective-permute-start.5 = (bf16[512,256]{1,0:T(8,128)(2,1)S(1)}, bf16[512,256]{1,0:T(8,128)(2,1)S(1)}, u32[]{:S(2)}, u32[]{:S(2)}) collective-permute-start(bf16[512,256]{1,0:T(8,128)(2,1)S(1)} %join.1.refs_0_), channel_id=1, source_target_pairs={{0,192},{64,0},{128,64},{192,128},{1,193},{65,1},{129,65},{193,129... | collective-permute-start | bytes 786440 | tf_op jit(solution)/shard_map/ppermute | solution.py:257
  12.2 0.0 collective-permute-done.q_other
  12.2 0.0 collective-permute-done.1.g_other
  12.2 0.0 copy-start
  12.2 0.9 %copy-done = bf16[128,1024]{1,0:T(8,128)(2,1)S(1)} copy-done((bf16[128,1024]{1,0:T(8,128)(2,1)S(1)}, bf16[128,1024]{1,0:T(8,128)(2,1)}, u32[]{:S(2)}) %copy-start) | copy-done | bytes 262168
  13.2 0.0 copy-start.1
  13.2 0.9 %copy-done.1 = bf16[128,1024]{1,0:T(8,128)(2,1)S(1)} copy-done((bf16[128,1024]{1,0:T(8,128)(2,1)S(1)}, bf16[128,1024]{1,0:T(8,128)(2,1)}, u32[]{:S(2)}) %copy-start.1) | copy-done | bytes 262168
  14.1 0.0 copy-start.2
  14.1 0.7 copy-done.2
  14.8 1.4 %prep.1 = (s32[36]{0:T(128)S(1)}, bf16[2,2048,128]{2,1,0:T(8,128)(2,1)S(1)}) custom-call(s32[64]{0:T(128)S(1)} %copy-done.2, s32[1]{0:T(128)} %bitcast.place, bf16[128,1024]{1,0:T(8,128)(2,1)S(1)} %copy-done, bf16[128,1024]{1,0:T(8,128)(2,1)S(1)} %collective-permute-done.q_other, bf16[128,1024]{1,0:T(8,128)(2,1)S(1)} %copy-done.1, ...), custom_call_target="tpu_custom_call" | custom-call | bytes 1048576 | tf_op jit(solution)/shard_map/prep/pallas_call | solution.py:40
  16.2 0.4 collective-permute-done.7.refs_0_.refs_1_
  16.6 0.1 collective-permute-start.8
  16.7 0.0 collective-permute-done.5.refs_0_.refs_2_
  16.7 3.5 %collective-permute-start.6 = (bf16[256,256]{1,0:T(8,128)(2,1)S(1)}, bf16[256,256]{1,0:T(8,128)(2,1)S(1)}, u32[]{:S(2)}, u32[]{:S(2)}) collective-permute-start(bf16[256,256]{1,0:T(8,128)(2,1)S(1)} %slice.20), channel_id=1, source_target_pairs={{0,192},{64,0},{128,64},{192,128},{1,193},{65,1},{129,65},{193,129... | collective-permute-start | bytes 393224 | tf_op jit(solution)/shard_map/ppermute | solution.py:257
  20.2 2.1 %stats.4 = (f32[8,2048]{1,0:T(8,128)S(1)}, f32[512,2048]{1,0:T(8,128)S(1)}, f32[512,2048]{1,0:T(8,128)S(1)}) custom-call(s32[36]{0:T(128)S(1)} %get-tuple-element.29.meta, bf16[2,2048,128]{2,1,0:T(8,128)(2,1)S(1)} %get-tuple-element.30.rows_qg, bf16[512,256]{1,0:T(8,128)(2,1)S(1)} %join.1.refs_0_), custom_call_target="tpu_custom_call" | custom-call | flops 536870912 | bytes 1048576 | tf_op jit(solution)/shard_map/stats/pallas_call | solution.py:40
  22.3 2.1 %stats.5 = (f32[8,2048]{1,0:T(8,128)S(1)}, f32[512,2048]{1,0:T(8,128)S(1)}, f32[512,2048]{1,0:T(8,128)S(1)}) custom-call(s32[36]{0:T(128)S(1)} %get-tuple-element.29.meta, bf16[2,2048,128]{2,1,0:T(8,128)(2,1)S(1)} %get-tuple-element.30.rows_qg, bf16[512,256]{1,0:T(8,128)(2,1)S(1)} %collective-permute-done.7.refs_0_.refs_1_, ...), custom_call_target="tpu_custom_call" | custom-call | flops 536870912 | bytes 1048576 | tf_op jit(solution)/shard_map/stats/pallas_call | solution.py:40
  24.3 2.1 %stats.6 = (f32[8,2048]{1,0:T(8,128)S(1)}, f32[512,2048]{1,0:T(8,128)S(1)}, f32[512,2048]{1,0:T(8,128)S(1)}) custom-call(s32[36]{0:T(128)S(1)} %get-tuple-element.29.meta, bf16[2,2048,128]{2,1,0:T(8,128)(2,1)S(1)} %get-tuple-element.30.rows_qg, bf16[512,256]{1,0:T(8,128)(2,1)S(1)} %collective-permute-done.5.refs_0_.refs_2_, ...), custom_call_target="tpu_custom_call" | custom-call | flops 536870912 | bytes 1048576 | tf_op jit(solution)/shard_map/stats/pallas_call | solution.py:40
  26.4 0.0 collective-permute-done.8.refs_1_.refs_4_
  26.4 0.0 collective-permute-done.6.refs_0_.refs_3_
  26.4 2.2 %stats.7 = (f32[8,2048]{1,0:T(8,128)S(1)}, f32[512,2048]{1,0:T(8,128)S(1)}, f32[512,2048]{1,0:T(8,128)S(1)}) custom-call(s32[36]{0:T(128)S(1)} %get-tuple-element.29.meta, bf16[2,2048,128]{2,1,0:T(8,128)(2,1)S(1)} %get-tuple-element.30.rows_qg, bf16[256,256]{1,0:T(8,128)(2,1)S(1)} %collective-permute-done.6.refs_0_.refs_3_, ...), custom_call_target="tpu_custom_call" | custom-call | flops 536870912 | bytes 1048576 | tf_op jit(solution)/shard_map/stats/pallas_call | solution.py:40
  28.6 0.1 collective-permute-start.9
  28.7 1.2 %collective-permute-done.9.came = f32[8,2048]{1,0:T(8,128)S(1)} collective-permute-done((f32[8,2048]{1,0:T(8,128)S(1)}, f32[8,2048]{1,0:T(8,128)S(1)}, u32[]{:S(2)}, u32[]{:S(2)}) %collective-permute-start.9) | collective-permute-done | bytes 65568 | tf_op jit(solution)/shard_map/ppermute | solution.py:254
  29.9 1.4 %grads.7 = (bf16[256,256]{1,0:T(8,128)(2,1)S(1)}, bf16[256,256]{1,0:T(8,128)(2,1)S(1)}) custom-call(bf16[2,2048,128]{2,1,0:T(8,128)(2,1)S(1)} %get-tuple-element.30.rows_qg, f32[8,2048]{1,0:T(8,128)S(1)} %get-tuple-element.34.final.refs_14_.own, f32[512,2048]{1,0:T(8,128)S(1)} %get-tuple-element.41.refs_15_.p_all, ...), custom_call_target="tpu_custom_call" | custom-call | flops 536870912 | bytes 1048576 | tf_op jit(solution)/shard_map/grads/pallas_call | solution.py:40
  31.3 0.2 collective-permute-start.11
  31.5 1.9 %collective-permute-start.12 = (bf16[256,256]{1,0:T(8,128)(2,1)S(1)}, bf16[256,256]{1,0:T(8,128)(2,1)S(1)}, u32[]{:S(2)}, u32[]{:S(2)}) collective-permute-start(bf16[256,256]{1,0:T(8,128)(2,1)S(1)} %get-tuple-element.46), channel_id=1, source_target_pairs={{0,64},{64,128},{128,192},{192,0},{1,65},{65,129},{129,193},{193,1... | collective-permute-start | bytes 393224 | tf_op jit(solution)/shard_map/ppermute | solution.py:257
  33.4 1.4 %grads.6.b = f32[512,256]{1,0:T(8,128)S(1)} custom-call(bf16[2,2048,128]{2,1,0:T(8,128)(2,1)S(1)} %get-tuple-element.30.rows_qg, f32[8,2048]{1,0:T(8,128)S(1)} %get-tuple-element.33.refs_2_.refs_11_.own, f32[512,2048]{1,0:T(8,128)S(1)} %get-tuple-element.39.refs_12_.p_all, f32[512,2048]{1,0:T(8,128)S(1)} %get-tuple-element.40.refs_13_.dp_all, ...), custom_call_target="tpu_custom_call" | custom-call | flops 536870912 | bytes 1048576 | tf_op jit(solution)/shard_map/grads/pallas_call | solution.py:40
  34.8 1.4 %grads.5.a = f32[512,256]{1,0:T(8,128)S(1)} custom-call(bf16[2,2048,128]{2,1,0:T(8,128)(2,1)S(1)} %get-tuple-element.30.rows_qg, f32[8,2048]{1,0:T(8,128)S(1)} %get-tuple-element.32.refs_1_.refs_8_.own, f32[512,2048]{1,0:T(8,128)S(1)} %get-tuple-element.37.refs_9_.p_all, f32[512,2048]{1,0:T(8,128)S(1)} %get-tuple-element.38.refs_10_.dp_all, ...), custom_call_target="tpu_custom_call" | custom-call | flops 536870912 | bytes 1048576 | tf_op jit(solution)/shard_map/grads/pallas_call | solution.py:40
  36.1 0.8 %collective-permute-done.11.to_a = bf16[256,256]{1,0:T(8,128)(2,1)S(1)} collective-permute-done((bf16[256,256]{1,0:T(8,128)(2,1)S(1)}, bf16[256,256]{1,0:T(8,128)(2,1)S(1)}, u32[]{:S(2)}, u32[]{:S(2)}) %collective-permute-start.11) | collective-permute-done | bytes 131104 | tf_op jit(solution)/shard_map/ppermute | solution.py:257
  36.9 1.5 %collective-permute-done.12.to_b = bf16[256,256]{1,0:T(8,128)(2,1)S(1)} collective-permute-done((bf16[256,256]{1,0:T(8,128)(2,1)S(1)}, bf16[256,256]{1,0:T(8,128)(2,1)S(1)}, u32[]{:S(2)}, u32[]{:S(2)}) %collective-permute-start.12) | collective-permute-done | bytes 131104 | tf_op jit(solution)/shard_map/ppermute | solution.py:257
  38.5 0.1 add_far.1
  38.5 0.1 collective-permute-start.13
  38.6 2.0 %collective-permute-start.14 = (bf16[512,256]{1,0:T(8,128)(2,1)S(1)}, bf16[512,256]{1,0:T(8,128)(2,1)S(1)}, u32[]{:S(2)}, u32[]{:S(2)}) collective-permute-start(bf16[512,256]{1,0:T(8,128)(2,1)S(1)} %get-tuple-element.48), channel_id=1, source_target_pairs={{0,64},{64,128},{128,192},{192,0},{1,65},{65,129},{129,193},{193,1... | collective-permute-start | bytes 786440 | tf_op jit(solution)/shard_map/ppermute | solution.py:257
  40.6 3.4 %queries.1 = (f32[128,1024]{1,0:T(8,128)S(1)}, f32[128,1024]{1,0:T(8,128)S(1)}) custom-call(f32[8,2048]{1,0:T(8,128)S(1)} %get-tuple-element.34.final.refs_14_.own, f32[8,2048]{1,0:T(8,128)S(1)} %collective-permute-done.9.came, bf16[512,256]{1,0:T(8,128)(2,1)S(1)} %join.1.refs_0_, bf16[512,256]{1,0:T(8,128)(2,1)S(1)} %collective-permute-done.7.refs_0_.refs_1_, ...), custom_call_target="tpu_custom_call" | custom-call | flops 1073741824 | bytes 1048576 | tf_op jit(solution)/shard_map/queries/pallas_call | solution.py:40
  44.0 0.1 collective-permute-start.10
  44.1 1.4 %grads.4.own = f32[512,256]{1,0:T(8,128)S(1)} custom-call(bf16[2,2048,128]{2,1,0:T(8,128)(2,1)S(1)} %get-tuple-element.30.rows_qg, f32[8,2048]{1,0:T(8,128)S(1)} %get-tuple-element.31.refs_1_.refs_5_.own, f32[512,2048]{1,0:T(8,128)S(1)} %get-tuple-element.35.refs_6_.p_all, f32[512,2048]{1,0:T(8,128)S(1)} %get-tuple-element.36.refs_7_.dp_all, ...), custom_call_target="tpu_custom_call" | custom-call | flops 536870912 | bytes 1048576 | tf_op jit(solution)/shard_map/grads/pallas_call | solution.py:40
  45.5 0.6 collective-permute-done.13.a
  46.1 1.3 %collective-permute-done.14.b = bf16[512,256]{1,0:T(8,128)(2,1)S(1)} collective-permute-done((bf16[512,256]{1,0:T(8,128)(2,1)S(1)}, bf16[512,256]{1,0:T(8,128)(2,1)S(1)}, u32[]{:S(2)}, u32[]{:S(2)}) %collective-permute-start.14) | collective-permute-done | bytes 262176 | tf_op jit(solution)/shard_map/ppermute | solution.py:257
  47.4 0.1 add_near.1
  47.5 2.0 %collective-permute-start.15 = (bf16[128,256]{1,0:T(8,128)(2,1)S(1)}, bf16[128,256]{1,0:T(8,128)(2,1)S(1)}, u32[]{:S(2)}, u32[]{:S(2)}) collective-permute-start(bf16[128,256]{1,0:T(8,128)(2,1)S(1)} %get-tuple-element.50), channel_id=1, source_target_pairs={{0,48},{16,0},{32,16},{48,32},{1,49},{17,1},{33,17},{49,33},{2,50}... | collective-permute-start | bytes 196616 | tf_op jit(solution)/shard_map/ppermute | solution.py:257
  49.5 1.2 %collective-permute-start.16 = (bf16[128,256]{1,0:T(8,128)(2,1)S(1)}, bf16[128,256]{1,0:T(8,128)(2,1)S(1)}, u32[]{:S(2)}, u32[]{:S(2)}) collective-permute-start(bf16[128,256]{1,0:T(8,128)(2,1)S(1)} %get-tuple-element.51), channel_id=1, source_target_pairs={{0,32},{16,48},{32,0},{48,16},{1,33},{17,49},{33,1},{49,17},{2,34}... | collective-permute-start | bytes 196616 | tf_op jit(solution)/shard_map/ppermute | solution.py:257
  50.7 1.6 %collective-permute-start.17 = (bf16[128,256]{1,0:T(8,128)(2,1)S(1)}, bf16[128,256]{1,0:T(8,128)(2,1)S(1)}, u32[]{:S(2)}, u32[]{:S(2)}) collective-permute-start(bf16[128,256]{1,0:T(8,128)(2,1)S(1)} %get-tuple-element.52), channel_id=1, source_target_pairs={{0,16},{16,32},{32,48},{48,0},{1,17},{17,33},{33,49},{49,1},{2,18}... | collective-permute-start | bytes 196616 | tf_op jit(solution)/shard_map/ppermute | solution.py:257
  52.3 0.0 collective-permute-done.15
  52.3 3.0 %collective-permute-done.16 = bf16[128,256]{1,0:T(8,128)(2,1)S(1)} collective-permute-done((bf16[128,256]{1,0:T(8,128)(2,1)S(1)}, bf16[128,256]{1,0:T(8,128)(2,1)S(1)}, u32[]{:S(2)}, u32[]{:S(2)}) %collective-permute-start.16) | collective-permute-done | bytes 65568 | tf_op jit(solution)/shard_map/ppermute | solution.py:257
  55.3 0.0 collective-permute-done.17
  55.3 0.0 collective-permute-done.10
  55.3 0.1 add_convert_fusion
  55.4 19.5 %all_to_all.5 = bf16[8,16,1280]{2,1,0:T(8,128)(2,1)S(1)} all-to-all(bf16[8,16,1280]{2,1,0:T(8,128)(2,1)S(1)} %bitcast.16), channel_id=1, replica_groups=mesh['y'=4,'x'=4,'core'=2,'head'=8] {'head'}, dimensions={0} | all-to-all | bytes 655360 | tf_op jit(solution)/shard_map/all_to_all | solution.py:284
  75.0 0.7 pad_maximum_fusion.1
  (9 shorter events, 0.2 us)
Async XLA Ops:
  0.8 5.3 %collective-permute-start.4 = (bf16[128,256]{1,0:T(8,128)(2,1)S(1)}, bf16[128,256]{1,0:T(8,128)(2,1)S(1)}, u32[]{:S(2)}, u32[]{:S(2)}) collective-permute-start(bf16[128,256]{1,0:T(8,128)(2,1)S(1)} %pad_maximum_fusion.2.refs_0_), channel_id=1, source_target_pairs={{0,48},{16,0},{32,16},{48,32},{1,49},{17,1},{33,17},{49,33},{2,50}... | collective-permute-start | bytes 196616 | tf_op jit(solution)/shard_map/ppermute | solution.py:257
  3.1 5.8 %collective-permute-start.3 = (bf16[128,256]{1,0:T(8,128)(2,1)S(1)}, bf16[128,256]{1,0:T(8,128)(2,1)S(1)}, u32[]{:S(2)}, u32[]{:S(2)}) collective-permute-start(bf16[128,256]{1,0:T(8,128)(2,1)S(1)} %pad_maximum_fusion.2.refs_0_), channel_id=1, source_target_pairs={{0,32},{16,48},{32,0},{48,16},{1,33},{17,49},{33,1},{49,17},{2,34}... | collective-permute-start | bytes 196616 | tf_op jit(solution)/shard_map/ppermute | solution.py:257
  3.8 5.1 %collective-permute-start.2 = (bf16[128,256]{1,0:T(8,128)(2,1)S(1)}, bf16[128,256]{1,0:T(8,128)(2,1)S(1)}, u32[]{:S(2)}, u32[]{:S(2)}) collective-permute-start(bf16[128,256]{1,0:T(8,128)(2,1)S(1)} %pad_maximum_fusion.2.refs_0_), channel_id=1, source_target_pairs={{0,16},{16,32},{32,48},{48,0},{1,17},{17,33},{33,49},{49,1},{2,18}... | collective-permute-start | bytes 196616 | tf_op jit(solution)/shard_map/ppermute | solution.py:257
  5.6 6.6 %collective-permute-start = (bf16[128,1024]{1,0:T(8,128)(2,1)}, bf16[128,1024]{1,0:T(8,128)(2,1)S(1)}, u32[]{:S(2)}, u32[]{:S(2)}) collective-permute-start(bf16[128,1024]{1,0:T(8,128)(2,1)} %q_own.1), channel_id=1, source_target_pairs={{0,8},{8,0},{1,9},{9,1},{2,10},{10,2},{3,11},{11,3},{4,12},{12,4},... | collective-permute-start | bytes 786440 | tf_op jit(solution)/shard_map/ppermute | solution.py:254
  5.6 6.6 %collective-permute-start.1 = (bf16[128,1024]{1,0:T(8,128)(2,1)}, bf16[128,1024]{1,0:T(8,128)(2,1)S(1)}, u32[]{:S(2)}, u32[]{:S(2)}) collective-permute-start(bf16[128,1024]{1,0:T(8,128)(2,1)} %g_own.1), channel_id=1, source_target_pairs={{0,8},{8,0},{1,9},{9,1},{2,10},{10,2},{3,11},{11,3},{4,12},{12,4},... | collective-permute-start | bytes 786440 | tf_op jit(solution)/shard_map/ppermute | solution.py:254
  8.9 7.7 %collective-permute-start.7 = (bf16[512,256]{1,0:T(8,128)(2,1)S(1)}, bf16[512,256]{1,0:T(8,128)(2,1)S(1)}, u32[]{:S(2)}, u32[]{:S(2)}) collective-permute-start(bf16[512,256]{1,0:T(8,128)(2,1)S(1)} %join.1.refs_0_), channel_id=1, source_target_pairs={{0,64},{64,128},{128,192},{192,0},{1,65},{65,129},{129,193},{193,1... | collective-permute-start | bytes 786440 | tf_op jit(solution)/shard_map/ppermute | solution.py:257
  9.8 6.9 %collective-permute-start.5 = (bf16[512,256]{1,0:T(8,128)(2,1)S(1)}, bf16[512,256]{1,0:T(8,128)(2,1)S(1)}, u32[]{:S(2)}, u32[]{:S(2)}) collective-permute-start(bf16[512,256]{1,0:T(8,128)(2,1)S(1)} %join.1.refs_0_), channel_id=1, source_target_pairs={{0,192},{64,0},{128,64},{192,128},{1,193},{65,1},{129,65},{193,129... | collective-permute-start | bytes 786440 | tf_op jit(solution)/shard_map/ppermute | solution.py:257
  12.2 1.0 %copy-start = (bf16[128,1024]{1,0:T(8,128)(2,1)S(1)}, bf16[128,1024]{1,0:T(8,128)(2,1)}, u32[]{:S(2)}) copy-start(bf16[128,1024]{1,0:T(8,128)(2,1)} %q_own.1) | copy-start | bytes 786436
  13.2 0.9 %copy-start.1 = (bf16[128,1024]{1,0:T(8,128)(2,1)S(1)}, bf16[128,1024]{1,0:T(8,128)(2,1)}, u32[]{:S(2)}) copy-start(bf16[128,1024]{1,0:T(8,128)(2,1)} %g_own.1) | copy-start | bytes 786436
  14.1 0.7 copy-start.2
  16.6 9.8 %collective-permute-start.8 = (bf16[256,256]{1,0:T(8,128)(2,1)S(1)}, bf16[256,256]{1,0:T(8,128)(2,1)S(1)}, u32[]{:S(2)}, u32[]{:S(2)}) collective-permute-start(bf16[256,256]{1,0:T(8,128)(2,1)S(1)} %slice.21), channel_id=1, source_target_pairs={{0,64},{64,128},{128,192},{192,0},{1,65},{65,129},{129,193},{193,1... | collective-permute-start | bytes 393224 | tf_op jit(solution)/shard_map/ppermute | solution.py:257
  16.7 9.7 %collective-permute-start.6 = (bf16[256,256]{1,0:T(8,128)(2,1)S(1)}, bf16[256,256]{1,0:T(8,128)(2,1)S(1)}, u32[]{:S(2)}, u32[]{:S(2)}) collective-permute-start(bf16[256,256]{1,0:T(8,128)(2,1)S(1)} %slice.20), channel_id=1, source_target_pairs={{0,192},{64,0},{128,64},{192,128},{1,193},{65,1},{129,65},{193,129... | collective-permute-start | bytes 393224 | tf_op jit(solution)/shard_map/ppermute | solution.py:257
  28.6 1.3 %collective-permute-start.9 = (f32[8,2048]{1,0:T(8,128)S(1)}, f32[8,2048]{1,0:T(8,128)S(1)}, u32[]{:S(2)}, u32[]{:S(2)}) collective-permute-start(f32[8,2048]{1,0:T(8,128)S(1)} %get-tuple-element.34.final.refs_14_.own), channel_id=1, source_target_pairs={{0,8},{8,0},{1,9},{9,1},{2,10},{10,2},{3,11},{11,3},{4,12},{12,4},... | collective-permute-start | bytes 196616 | tf_op jit(solution)/shard_map/ppermute | solution.py:254
  31.3 5.6 %collective-permute-start.11 = (bf16[256,256]{1,0:T(8,128)(2,1)S(1)}, bf16[256,256]{1,0:T(8,128)(2,1)S(1)}, u32[]{:S(2)}, u32[]{:S(2)}) collective-permute-start(bf16[256,256]{1,0:T(8,128)(2,1)S(1)} %get-tuple-element.45), channel_id=1, source_target_pairs={{0,192},{64,0},{128,64},{192,128},{1,193},{65,1},{129,65},{193,129... | collective-permute-start | bytes 393224 | tf_op jit(solution)/shard_map/ppermute | solution.py:257
  31.5 7.0 %collective-permute-start.12 = (bf16[256,256]{1,0:T(8,128)(2,1)S(1)}, bf16[256,256]{1,0:T(8,128)(2,1)S(1)}, u32[]{:S(2)}, u32[]{:S(2)}) collective-permute-start(bf16[256,256]{1,0:T(8,128)(2,1)S(1)} %get-tuple-element.46), channel_id=1, source_target_pairs={{0,64},{64,128},{128,192},{192,0},{1,65},{65,129},{129,193},{193,1... | collective-permute-start | bytes 393224 | tf_op jit(solution)/shard_map/ppermute | solution.py:257
  38.5 7.6 %collective-permute-start.13 = (bf16[512,256]{1,0:T(8,128)(2,1)S(1)}, bf16[512,256]{1,0:T(8,128)(2,1)S(1)}, u32[]{:S(2)}, u32[]{:S(2)}) collective-permute-start(bf16[512,256]{1,0:T(8,128)(2,1)S(1)} %get-tuple-element.47), channel_id=1, source_target_pairs={{0,192},{64,0},{128,64},{192,128},{1,193},{65,1},{129,65},{193,129... | collective-permute-start | bytes 786440 | tf_op jit(solution)/shard_map/ppermute | solution.py:257
  38.6 8.8 %collective-permute-start.14 = (bf16[512,256]{1,0:T(8,128)(2,1)S(1)}, bf16[512,256]{1,0:T(8,128)(2,1)S(1)}, u32[]{:S(2)}, u32[]{:S(2)}) collective-permute-start(bf16[512,256]{1,0:T(8,128)(2,1)S(1)} %get-tuple-element.48), channel_id=1, source_target_pairs={{0,64},{64,128},{128,192},{192,0},{1,65},{65,129},{129,193},{193,1... | collective-permute-start | bytes 786440 | tf_op jit(solution)/shard_map/ppermute | solution.py:257
  44.0 11.3 %collective-permute-start.10 = (f32[128,1024]{1,0:T(8,128)S(1)}, f32[128,1024]{1,0:T(8,128)S(1)}, u32[]{:S(2)}, u32[]{:S(2)}) collective-permute-start(f32[128,1024]{1,0:T(8,128)S(1)} %get-tuple-element.44), channel_id=1, source_target_pairs={{0,8},{8,0},{1,9},{9,1},{2,10},{10,2},{3,11},{11,3},{4,12},{12,4},... | collective-permute-start | bytes 1572872 | tf_op jit(solution)/shard_map/ppermute | solution.py:254
  47.5 4.7 %collective-permute-start.15 = (bf16[128,256]{1,0:T(8,128)(2,1)S(1)}, bf16[128,256]{1,0:T(8,128)(2,1)S(1)}, u32[]{:S(2)}, u32[]{:S(2)}) collective-permute-start(bf16[128,256]{1,0:T(8,128)(2,1)S(1)} %get-tuple-element.50), channel_id=1, source_target_pairs={{0,48},{16,0},{32,16},{48,32},{1,49},{17,1},{33,17},{49,33},{2,50}... | collective-permute-start | bytes 196616 | tf_op jit(solution)/shard_map/ppermute | solution.py:257
  49.5 5.8 %collective-permute-start.16 = (bf16[128,256]{1,0:T(8,128)(2,1)S(1)}, bf16[128,256]{1,0:T(8,128)(2,1)S(1)}, u32[]{:S(2)}, u32[]{:S(2)}) collective-permute-start(bf16[128,256]{1,0:T(8,128)(2,1)S(1)} %get-tuple-element.51), channel_id=1, source_target_pairs={{0,32},{16,48},{32,0},{48,16},{1,33},{17,49},{33,1},{49,17},{2,34}... | collective-permute-start | bytes 196616 | tf_op jit(solution)/shard_map/ppermute | solution.py:257
  50.7 4.6 %collective-permute-start.17 = (bf16[128,256]{1,0:T(8,128)(2,1)S(1)}, bf16[128,256]{1,0:T(8,128)(2,1)S(1)}, u32[]{:S(2)}, u32[]{:S(2)}) collective-permute-start(bf16[128,256]{1,0:T(8,128)(2,1)S(1)} %get-tuple-element.52), channel_id=1, source_target_pairs={{0,16},{16,32},{32,48},{48,0},{1,17},{17,33},{33,49},{49,1},{2,18}... | collective-permute-start | bytes 196616 | tf_op jit(solution)/shard_map/ppermute | solution.py:257
